TPU v7x, 256 devices: a whole 4x4x8 slice. The times are simulated.
256 devices in a mesh: frame: 8 (over x_lo, y), patch: 32 (over z, x_hi, core).
Axes of the slice: x: 4 (x_hi: 2, x_lo: 2; x = x_hi * 2 + x_lo), y: 4, z: 8, core: 2. Of those that a mesh axis runs over, the one named last changes fastest.
Arguments:
- latent: bfloat16 [16, 64, 112, 320], P('frame', 'patch'), may hold values from -24 to 24
- timestep: int32 [1], replicated, may hold values from 0 to 24
- time_weight: bfloat16 [320, 320], replicated, may hold values from -0.3125 to 0.3125
- norm_gain: float32 [320], replicated, may hold values from 0.1 to 1.9
- norm_bias: float32 [320], replicated, may hold values from -3 to 3
- spatial_qkv: bfloat16 [320, 960], replicated, may hold values from -2 to 2
- spatial_out: bfloat16 [320, 320], replicated, may hold values from -0.3125 to 0.3125
- stale_codes: bfloat16 [16, 64, 112, 320], P('frame', 'patch'), may hold values from -8 to 8
- stale_exponents: int32 [16, 64, 5], P('frame', 'patch'), may hold values from -1 to 2
- temporal_qkv: bfloat16 [320, 960], replicated, may hold values from -2 to 2
- temporal_out: bfloat16 [320, 320], replicated, may hold values from -0.3125 to 0.3125
Outputs:
- block_output: bfloat16 [16, 64, 112, 320], P('frame', 'patch')
- residual_codes: bfloat16 [16, 64, 112, 320], P('frame', 'patch')
All inputs are finite; a program needn't handle non-finite values.
Results may differ from a plain program's by a relative error of at most 0.02.
The roundings to bfloat16 on the way count: a program that leaves them out, or rounds other values in their place, can miss the bound.
Values may be sent and summed in bfloat16 or wider, within the bound.
A program may use at most 128 MiB of HBM per device.

v0:
```python
import math

import jax
import jax.numpy as jnp
from jax import lax
from jax.sharding import PartitionSpec as P

HEAD = 64
GROUPS = 32


def sinusoid(position, channels):
    half_width = channels // 2
    frequency = jnp.exp(-math.log(10000.0) * jnp.arange(half_width, dtype=jnp.float32) / half_width)
    angles = position[..., None] * frequency
    return jnp.concatenate([jnp.cos(angles), jnp.sin(angles)], axis=-1)


def split_heads(values, head_size):
    frame_count, row_count, column_count, channels = values.shape
    shaped = values.reshape(frame_count, row_count * column_count, channels // head_size, head_size)
    return jnp.transpose(shaped, (2, 0, 1, 3))


def empty_state(head_count, frame_count, query_count, head_size):
    return (
        jnp.full((head_count, frame_count, query_count), -1e30, jnp.float32),
        jnp.zeros((head_count, frame_count, query_count), jnp.float32),
        jnp.zeros((head_count, frame_count, query_count, head_size), jnp.float32),
    )


def fold_heads(state_in, query_heads, key_heads, value_heads, key_mask, scaling):

    def one_head(operands):
        head_peaks, head_totals, head_sums, query_one, key_one, value_one = operands
        scores = (
            jnp.einsum("fqd,fkd->fqk", query_one, key_one, preferred_element_type=jnp.float32)
            * scaling
        )
        scores = jnp.where(key_mask, -1e30, scores)
        new_peaks = jnp.maximum(head_peaks, jnp.max(scores, axis=-1))
        keep_share = jnp.exp(head_peaks - new_peaks)
        weights = jnp.exp(scores - new_peaks[..., None])
        new_totals = head_totals * keep_share + jnp.sum(weights, axis=-1)
        new_sums = head_sums * keep_share[..., None] + jnp.einsum(
            "fqk,fkd->fqd",
            weights.astype(jnp.bfloat16),
            value_one,
            preferred_element_type=jnp.float32,
        )
        return (new_peaks, new_totals, new_sums)

    return lax.map(
        one_head, (state_in[0], state_in[1], state_in[2], query_heads, key_heads, value_heads)
    )


def block_rows(piece_rows, band_rows, columns_dev):
    return band_rows * math.gcd(piece_rows // band_rows, max(1, 1024 // (band_rows * columns_dev)))


def project_pairs(stale_part, key_weight):
    frame_count, row_count, column_count, channels = stale_part.shape
    flat = jnp.dot(stale_part.reshape(-1, channels), key_weight, preferred_element_type=jnp.float32)
    return flat.astype(jnp.bfloat16).reshape(
        frame_count, row_count, column_count, key_weight.shape[1]
    )


def body(
    latent,
    timestep,
    time_weight,
    norm_gain,
    norm_bias,
    spatial_qkv,
    spatial_out,
    stale_codes,
    stale_exponents,
    temporal_qkv,
    temporal_out,
):
    frames, band_rows, columns_dev, channels = latent.shape
    head_size = HEAD
    head_count = channels // head_size
    scaling = head_size ** (-0.5)
    patch_count = lax.axis_size("patch")
    my_band = lax.axis_index("patch")
    query_count = band_rows * columns_dev
    time_embed = sinusoid(timestep.astype(jnp.float32), channels).astype(jnp.bfloat16)
    time_shift = jnp.dot(time_embed, time_weight, preferred_element_type=jnp.float32)[0]
    latent_wide = latent.astype(jnp.float32)
    group_width = channels // GROUPS
    grouped = latent_wide.reshape(frames, query_count, GROUPS, group_width)
    cell_count = band_rows * patch_count * columns_dev * group_width
    group_mean = lax.psum(jnp.sum(grouped, axis=(1, 3), keepdims=True), "patch") / cell_count
    centered = grouped - group_mean
    group_var = (
        lax.psum(jnp.sum(centered * centered, axis=(1, 3), keepdims=True), "patch") / cell_count
    )
    normed = (centered * lax.rsqrt(group_var + 1e-05)).reshape(
        frames, band_rows, columns_dev, channels
    )
    normed_in = (normed * norm_gain + norm_bias + time_shift).astype(jnp.bfloat16)
    projected = jnp.dot(
        normed_in.reshape(-1, channels), spatial_qkv, preferred_element_type=jnp.float32
    ).reshape(frames, band_rows, columns_dev, 3 * channels)
    query_rows = projected[..., :channels].astype(jnp.bfloat16)
    fresh_kv = projected[..., channels:].astype(jnp.bfloat16)
    key_weight = spatial_qkv[:, channels:]
    factor_bf = jnp.exp2(stale_exponents.astype(jnp.float32)).astype(jnp.bfloat16)
    factor_full = jnp.repeat(factor_bf.astype(jnp.float32), head_size, axis=-1)[:, :, None, :]
    stale_local = (stale_codes.astype(jnp.float32) * factor_full).astype(jnp.bfloat16)
    residual_codes = (
        (normed_in.astype(jnp.float32) - stale_local.astype(jnp.float32)) / factor_full
    ).astype(jnp.bfloat16)
    query_heads = split_heads(query_rows, head_size)
    no_mask = jnp.zeros((query_count,), jnp.bool_)
    fresh_part = fold_heads(
        empty_state(head_count, frames, query_count, head_size),
        query_heads,
        split_heads(fresh_kv[..., :channels], head_size),
        split_heads(fresh_kv[..., channels:], head_size),
        no_mask,
        scaling,
    )

    def masked_fold(state_now, pairs, row_first):
        row_owner = (row_first + jnp.arange(pairs.shape[1], dtype=jnp.int32)) // band_rows
        key_mask = jnp.repeat(row_owner == my_band, columns_dev)
        return fold_heads(
            state_now,
            query_heads,
            split_heads(pairs[..., :channels], head_size),
            split_heads(pairs[..., channels:], head_size),
            key_mask,
            scaling,
        )

    code_piece = lax.all_gather(stale_codes, "patch", axis=1, tiled=True)
    factor_piece = lax.all_gather(factor_bf, "patch", axis=1, tiled=True)
    piece_rows = code_piece.shape[1]
    step_rows = block_rows(piece_rows, band_rows, columns_dev)

    def one_block(block_index, state_now):
        row_start = block_index * step_rows
        codes = lax.dynamic_slice_in_dim(code_piece, row_start, step_rows, 1)
        factors = lax.dynamic_slice_in_dim(factor_piece, row_start, step_rows, 1)
        block_scale = jnp.repeat(factors.astype(jnp.float32), head_size, axis=-1)[:, :, None, :]
        decoded = (codes.astype(jnp.float32) * block_scale).astype(jnp.bfloat16)
        return masked_fold(state_now, project_pairs(decoded, key_weight), row_start)

    state_out = lax.fori_loop(0, piece_rows // step_rows, one_block, fresh_part)
    head_sums = state_out[2] / state_out[1][..., None]
    attended = (
        jnp.transpose(head_sums, (1, 2, 0, 3))
        .reshape(frames, band_rows, columns_dev, channels)
        .astype(jnp.bfloat16)
    )
    mixed_rows = jnp.dot(
        attended.reshape(-1, channels), spatial_out, preferred_element_type=jnp.float32
    ).reshape(frames, band_rows, columns_dev, channels)
    section_one = lax.optimization_barrier((latent_wide + mixed_rows).astype(jnp.bfloat16))
    frame_index = (lax.axis_index("frame") * frames + jnp.arange(frames, dtype=jnp.int32)).astype(
        jnp.float32
    )
    shifted = section_one.astype(jnp.float32) + sinusoid(frame_index, channels)[:, None, None, :]
    row_mean = jnp.mean(shifted, axis=-1, keepdims=True)
    deviation = shifted - row_mean
    normed_t = (
        deviation * lax.rsqrt(jnp.mean(deviation * deviation, axis=-1, keepdims=True) + 1e-05)
    ).astype(jnp.bfloat16)
    frame_block = lax.all_to_all(normed_t, "frame", split_axis=2, concat_axis=0, tiled=True)
    frame_count, item_count, column_count, _ = frame_block.shape
    temporal_proj = jnp.dot(
        frame_block.reshape(-1, channels), temporal_qkv, preferred_element_type=jnp.float32
    ).astype(jnp.bfloat16)
    temporal_proj = temporal_proj.reshape(
        frame_count, item_count * column_count, 3, head_count, head_size
    )
    scores = (
        jnp.einsum(
            "fphd,gphd->phfg",
            temporal_proj[:, :, 0],
            temporal_proj[:, :, 1],
            preferred_element_type=jnp.float32,
        )
        * scaling
    )
    weights = jnp.exp(scores - jnp.max(scores, axis=-1, keepdims=True))
    denominator = jnp.sum(weights, axis=-1)
    numerator = jnp.einsum(
        "phfg,gphd->fphd",
        weights.astype(jnp.bfloat16),
        temporal_proj[:, :, 2],
        preferred_element_type=jnp.float32,
    )
    mixed_t = (numerator / jnp.transpose(denominator, (2, 0, 1))[..., None]).astype(jnp.bfloat16)
    mixed_t = mixed_t.reshape(frame_count, item_count, column_count, channels)
    temporal_mix = lax.all_to_all(mixed_t, "frame", split_axis=0, concat_axis=2, tiled=True)
    temporal_rows = jnp.dot(
        temporal_mix.reshape(-1, channels), temporal_out, preferred_element_type=jnp.float32
    ).reshape(frames, band_rows, columns_dev, channels)
    block_output = (section_one.astype(jnp.float32) + temporal_rows).astype(jnp.bfloat16)
    return (block_output, residual_codes)


def solution(mesh):
    placed = (
        P("frame", "patch", None, None),
        P(),
        P(),
        P(),
        P(),
        P(),
        P(),
        P("frame", "patch", None, None),
        P("frame", "patch", None),
        P(),
        P(),
    )
    return jax.shard_map(
        body,
        mesh=mesh,
        in_specs=placed,
        out_specs=(P("frame", "patch", None, None), P("frame", "patch", None, None)),
        check_vma=False,
    )
```

profile of v0, /device:TPU:30, one launch (start us, length us, event | category | flops | bytes accessed | tf_op | source)
XLA Modules:
  0.0 511.3 jit_solution(2588657813307447083)
XLA Ops:
  7.3 2.0 copy.94
  10.7 67.8 %psum.14 = f32[2,1,32,1]{2,0,3,1:T(2,128)S(1)} all-reduce(f32[2,1,32,1]{2,0,3,1:T(2,128)S(1)} %bitcast.205), channel_id=1, replica_groups=mesh['frame'=8,'patch'=32] {'patch'}, use_global_device_ids=true, to_apply=%region_2.0 | all-reduce | flops 64 | bytes 512 | tf_op jit(solution)/shard_map/psum | solution.py:97
  79.2 65.5 %psum.15 = f32[2,1,32,1]{2,0,3,1:T(2,128)S(1)} all-reduce(f32[2,1,32,1]{2,0,3,1:T(2,128)S(1)} %bitcast.204), channel_id=1, replica_groups=mesh['frame'=8,'patch'=32] {'patch'}, use_global_device_ids=true, to_apply=%region_5.6 | all-reduce | flops 64 | bytes 512 | tf_op jit(solution)/shard_map/psum | solution.py:100
  149.9 42.3 %all_gather.7 = bf16[2,64,5]{2,0,1:T(2,128)(2,1)S(1)} all-gather(bf16[2,2,5]{2,0,1:T(2,128)(2,1)S(1)} %fusion.66), channel_id=1, replica_groups=mesh['frame'=8,'patch'=32] {'patch'}, dimensions={1}, use_global_device_ids=true | all-gather | bytes 1320 | tf_op jit(solution)/shard_map/all_gather | solution.py:142
  192.5 10.6 %while.69 = (s32[]{:T(128)}, f32[5,2,224]{2,1,0:T(2,128)S(1)}, f32[5,2,224]{2,1,0:T(2,128)S(1)}, f32[5,2,224,64]{2,3,1,0:T(8,128)}, bf16[5,2,224,64]{2,3,1,0:T(8...) while((s32[]{:T(128)}, f32[5,2,224]{2,1,0:T(2,128)S(1)}, ...), condition=%wide.region_9.10_spmd, body=%wide.region_6.9_spmd.sunk | while | flops 26323136 | bytes 1614425 | solution.py:54
  203.1 265.4 %while.71 = (s32[]{:T(128)}, f32[5,2,224]{2,1,0:T(2,128)S(1)}, f32[5,2,224]{2,1,0:T(2,128)S(1)}, f32[5,2,224,64]{2,3,1,0:T(8,128)}, bf16[2,64,112,320]{3,2,1,0:T...) while((s32[]{:T(128)}, f32[5,2,224]{2,1,0:T(2,128)S(1)}, ...), condition=%wide.region_15.16_spmd, body=%wide.region_10.15_spmd.sunk | while | flops 842500032 | bytes 29134116 | solution.py:154
  207.2 1.8 copy.158
  209.0 3.5 reshape.226
  214.7 21.5 %while.72 = (s32[]{:T(128)}, f32[5,2,224]{2,1,0:T(2,128)S(1)}, f32[5,2,224]{2,1,0:T(2,128)S(1)}, f32[5,2,224,64]{2,3,1,0:T(8,128)}, bf16[5,2,224,64]{2,3,1,0:T(8...) while((s32[]{:T(128)}, f32[5,2,224]{2,1,0:T(2,128)S(1)}, ...), condition=%wide.region_14.14_spmd.clone.clone, body=%wide.region_11.13_spmd.clone.clone.sunk | while | flops 105629440 | bytes 5867377 | solution.py:54
  240.3 1.8 copy.158
  242.1 3.5 reshape.226
  247.9 21.5 %while.72 = (s32[]{:T(128)}, f32[5,2,224]{2,1,0:T(2,128)S(1)}, f32[5,2,224]{2,1,0:T(2,128)S(1)}, f32[5,2,224,64]{2,3,1,0:T(8,128)}, bf16[5,2,224,64]{2,3,1,0:T(8...) while((s32[]{:T(128)}, f32[5,2,224]{2,1,0:T(2,128)S(1)}, ...), condition=%wide.region_14.14_spmd.clone.clone, body=%wide.region_11.13_spmd.clone.clone.sunk | while | flops 105629440 | bytes 5867377 | solution.py:54
  275.3 3.5 reshape.226
  281.1 21.5 %while.72 = (s32[]{:T(128)}, f32[5,2,224]{2,1,0:T(2,128)S(1)}, f32[5,2,224]{2,1,0:T(2,128)S(1)}, f32[5,2,224,64]{2,3,1,0:T(8,128)}, bf16[5,2,224,64]{2,3,1,0:T(8...) while((s32[]{:T(128)}, f32[5,2,224]{2,1,0:T(2,128)S(1)}, ...), condition=%wide.region_14.14_spmd.clone.clone, body=%wide.region_11.13_spmd.clone.clone.sunk | while | flops 105629440 | bytes 5867377 | solution.py:54
  306.7 1.8 copy.158
  308.5 3.5 reshape.226
  314.3 21.5 %while.72 = (s32[]{:T(128)}, f32[5,2,224]{2,1,0:T(2,128)S(1)}, f32[5,2,224]{2,1,0:T(2,128)S(1)}, f32[5,2,224,64]{2,3,1,0:T(8,128)}, bf16[5,2,224,64]{2,3,1,0:T(8...) while((s32[]{:T(128)}, f32[5,2,224]{2,1,0:T(2,128)S(1)}, ...), condition=%wide.region_14.14_spmd.clone.clone, body=%wide.region_11.13_spmd.clone.clone.sunk | while | flops 105629440 | bytes 5867377 | solution.py:54
  339.8 1.8 copy.158
  341.7 3.5 reshape.226
  347.4 21.5 %while.72 = (s32[]{:T(128)}, f32[5,2,224]{2,1,0:T(2,128)S(1)}, f32[5,2,224]{2,1,0:T(2,128)S(1)}, f32[5,2,224,64]{2,3,1,0:T(8,128)}, bf16[5,2,224,64]{2,3,1,0:T(8...) while((s32[]{:T(128)}, f32[5,2,224]{2,1,0:T(2,128)S(1)}, ...), condition=%wide.region_14.14_spmd.clone.clone, body=%wide.region_11.13_spmd.clone.clone.sunk | while | flops 105629440 | bytes 5867377 | solution.py:54
  374.8 3.5 reshape.226
  380.6 21.5 %while.72 = (s32[]{:T(128)}, f32[5,2,224]{2,1,0:T(2,128)S(1)}, f32[5,2,224]{2,1,0:T(2,128)S(1)}, f32[5,2,224,64]{2,3,1,0:T(8,128)}, bf16[5,2,224,64]{2,3,1,0:T(8...) while((s32[]{:T(128)}, f32[5,2,224]{2,1,0:T(2,128)S(1)}, ...), condition=%wide.region_14.14_spmd.clone.clone, body=%wide.region_11.13_spmd.clone.clone.sunk | while | flops 105629440 | bytes 5867377 | solution.py:54
  406.2 1.8 copy.158
  408.0 3.5 reshape.226
  413.8 21.5 %while.72 = (s32[]{:T(128)}, f32[5,2,224]{2,1,0:T(2,128)S(1)}, f32[5,2,224]{2,1,0:T(2,128)S(1)}, f32[5,2,224,64]{2,3,1,0:T(8,128)}, bf16[5,2,224,64]{2,3,1,0:T(8...) while((s32[]{:T(128)}, f32[5,2,224]{2,1,0:T(2,128)S(1)}, ...), condition=%wide.region_14.14_spmd.clone.clone, body=%wide.region_11.13_spmd.clone.clone.sunk | while | flops 105629440 | bytes 5867377 | solution.py:54
  439.4 1.8 copy.158
  441.2 3.5 reshape.226
  446.9 21.5 %while.72 = (s32[]{:T(128)}, f32[5,2,224]{2,1,0:T(2,128)S(1)}, f32[5,2,224]{2,1,0:T(2,128)S(1)}, f32[5,2,224,64]{2,3,1,0:T(8,128)}, bf16[5,2,224,64]{2,3,1,0:T(8...) while((s32[]{:T(128)}, f32[5,2,224]{2,1,0:T(2,128)S(1)}, ...), condition=%wide.region_14.14_spmd.clone.clone, body=%wide.region_11.13_spmd.clone.clone.sunk | while | flops 105629440 | bytes 5867377 | solution.py:54
  471.7 11.3 %all_to_all.30 = bf16[2,2,112,320]{3,1,0,2:T(2,128)(2,1)S(1)} all-to-all(bf16[2,2,112,320]{3,1,0,2:T(2,128)(2,1)S(1)} %copy.101), channel_id=1, replica_groups=mesh['frame'=8,'patch'=32] {'frame'}, dimensions={2} | all-to-all | bytes 573440 | tf_op jit(solution)/shard_map/all_to_all | solution.py:174
  484.8 3.1 reshape.210
  491.8 6.3 %all-to-all-start.1 = ((bf16[16,2,14,320]{3,1,2,0:T(2,128)(2,1)}), bf16[16,2,14,320]{3,1,2,0:T(2,128)(2,1)S(1)}, u32[]{:S(2)}, u32[]{:S(2)}) async-start(bf16[16,2,14,320]{3,1,2,0:T(2,128)(2,1)} %copy.109), calls=%async_computation.1 | async-start | bytes 688128 | tf_op jit(solution)/shard_map/all_to_all | solution.py:201
  499.5 3.6 all-to-all-done.1
  (550 shorter events, 253.3 us)
Async XLA Ops:
  7.2 476.0 %copy-start = (bf16[320,960]{1,0:T(8,128)(2,1)S(1)}, bf16[320,960]{1,0:T(8,128)(2,1)}, u32[]{:S(2)}) copy-start(bf16[320,960]{1,0:T(8,128)(2,1)} %param.26) | copy-start | bytes 1843204
  7.2 71.5 %copy-start.1 = (bf16[2,2,112,320]{2,3,1,0:T(8,128)(2,1)S(1)}, bf16[2,2,112,320]{2,3,1,0:T(8,128)(2,1)}, u32[]{:S(2)}) copy-start(bf16[2,2,112,320]{2,3,1,0:T(8,128)(2,1)} %param.17) | copy-start | bytes 860164
  7.2 138.5 %copy-start.6 = (bf16[320,960]{1,0:T(8,128)(2,1)S(1)}, bf16[320,960]{1,0:T(8,128)(2,1)}, u32[]{:S(2)}) copy-start(bf16[320,960]{1,0:T(8,128)(2,1)} %param.22) | copy-start | bytes 1843204
  7.2 138.7 %copy-start.12 = (bf16[320,320]{1,0:T(8,128)(2,1)S(1)}, bf16[320,320]{1,0:T(8,128)(2,1)}, u32[]{:S(2)}) copy-start(bf16[320,320]{1,0:T(8,128)(2,1)} %param.19) | copy-start | bytes 614404
  7.2 138.9 %copy-start.14 = (f32[320]{0:T(512)S(1)}, f32[320]{0:T(512)}, u32[]{:S(2)}) copy-start(f32[320]{0:T(512)} %param.20) | copy-start | bytes 3844
  7.2 138.9 %copy-start.13 = (f32[320]{0:T(512)S(1)}, f32[320]{0:T(512)}, u32[]{:S(2)}) copy-start(f32[320]{0:T(512)} %param.21) | copy-start | bytes 3844
  7.2 195.8 %all-gather.2.cloned.1.call-start = ((), (), s32[]{:S(2)}) async-start(), calls=%async_computation.2 | async-start | bytes 11354112 | tf_op jit(solution)/shard_map/all_gather | solution.py:141
  148.7 1.2 copy-start.15
  203.1 1.8 copy-start.8
  214.7 21.5 %copy-start.9 = (bf16[320,640]{1,0:T(8,128)(2,1)S(1)}, bf16[320,640]{1,0:T(8,128)(2,1)}, u32[]{:S(2)}) copy-start(bf16[320,640]{1,0:T(8,128)(2,1)} %copy-done.8) | copy-start | bytes 1228804 | tf_op jit(solution)/shard_map/while
  236.3 1.8 copy-start.8
  247.9 21.5 %copy-start.9 = (bf16[320,640]{1,0:T(8,128)(2,1)S(1)}, bf16[320,640]{1,0:T(8,128)(2,1)}, u32[]{:S(2)}) copy-start(bf16[320,640]{1,0:T(8,128)(2,1)} %copy-done.8) | copy-start | bytes 1228804 | tf_op jit(solution)/shard_map/while
  269.4 1.8 copy-start.8
  281.1 21.5 %copy-start.9 = (bf16[320,640]{1,0:T(8,128)(2,1)S(1)}, bf16[320,640]{1,0:T(8,128)(2,1)}, u32[]{:S(2)}) copy-start(bf16[320,640]{1,0:T(8,128)(2,1)} %copy-done.8) | copy-start | bytes 1228804 | tf_op jit(solution)/shard_map/while
  302.6 1.8 copy-start.8
  314.2 21.5 %copy-start.9 = (bf16[320,640]{1,0:T(8,128)(2,1)S(1)}, bf16[320,640]{1,0:T(8,128)(2,1)}, u32[]{:S(2)}) copy-start(bf16[320,640]{1,0:T(8,128)(2,1)} %copy-done.8) | copy-start | bytes 1228804 | tf_op jit(solution)/shard_map/while
  335.8 1.8 copy-start.8
  347.4 21.5 %copy-start.9 = (bf16[320,640]{1,0:T(8,128)(2,1)S(1)}, bf16[320,640]{1,0:T(8,128)(2,1)}, u32[]{:S(2)}) copy-start(bf16[320,640]{1,0:T(8,128)(2,1)} %copy-done.8) | copy-start | bytes 1228804 | tf_op jit(solution)/shard_map/while
  368.9 1.8 copy-start.8
  380.6 21.5 %copy-start.9 = (bf16[320,640]{1,0:T(8,128)(2,1)S(1)}, bf16[320,640]{1,0:T(8,128)(2,1)}, u32[]{:S(2)}) copy-start(bf16[320,640]{1,0:T(8,128)(2,1)} %copy-done.8) | copy-start | bytes 1228804 | tf_op jit(solution)/shard_map/while
  402.1 1.8 copy-start.8
  413.8 21.5 %copy-start.9 = (bf16[320,640]{1,0:T(8,128)(2,1)S(1)}, bf16[320,640]{1,0:T(8,128)(2,1)}, u32[]{:S(2)}) copy-start(bf16[320,640]{1,0:T(8,128)(2,1)} %copy-done.8) | copy-start | bytes 1228804 | tf_op jit(solution)/shard_map/while
  435.3 1.8 copy-start.8
  446.9 21.5 %copy-start.9 = (bf16[320,640]{1,0:T(8,128)(2,1)S(1)}, bf16[320,640]{1,0:T(8,128)(2,1)}, u32[]{:S(2)}) copy-start(bf16[320,640]{1,0:T(8,128)(2,1)} %copy-done.8) | copy-start | bytes 1228804 | tf_op jit(solution)/shard_map/while
  468.4 1.5 copy-start.2
  468.5 1.5 copy-start.10
  470.3 0.7 copy-start.4
  490.2 7.9 %copy-start.3 = (bf16[2,2,112,320]{2,3,1,0:T(8,128)(2,1)S(1)}, bf16[2,2,112,320]{2,3,1,0:T(8,128)(2,1)}, u32[]{:S(2)}) copy-start(bf16[2,2,112,320]{2,3,1,0:T(8,128)(2,1)} %param.17) | copy-start | bytes 860164
  490.3 7.9 %copy-start.7 = (bf16[2,2,112,320]{2,3,1,0:T(8,128)(2,1)S(1)}, bf16[2,2,112,320]{2,3,1,0:T(8,128)(2,1)}, u32[]{:S(2)}) copy-start(bf16[2,2,112,320]{2,3,1,0:T(8,128)(2,1)} %param.24) | copy-start | bytes 860164
  491.8 11.5 %copy-start.5 = (bf16[2,2,112,320]{2,3,1,0:T(8,128)(2,1)S(1)}, bf16[2,2,112,320]{2,3,1,0:T(8,128)(2,1)}, u32[]{:S(2)}) copy-start(bf16[2,2,112,320]{2,3,1,0:T(8,128)(2,1)} %copy-done.4) | copy-start | bytes 860164
  491.8 11.5 %copy-start.11 = (bf16[320,320]{1,0:T(8,128)(2,1)S(1)}, bf16[320,320]{1,0:T(8,128)(2,1)}, u32[]{:S(2)}) copy-start(bf16[320,320]{1,0:T(8,128)(2,1)} %param.27) | copy-start | bytes 614404
  491.8 11.3 %all-to-all-start.1 = ((bf16[16,2,14,320]{3,1,2,0:T(2,128)(2,1)}), bf16[16,2,14,320]{3,1,2,0:T(2,128)(2,1)S(1)}, u32[]{:S(2)}, u32[]{:S(2)}) async-start(bf16[16,2,14,320]{3,1,2,0:T(2,128)(2,1)} %copy.109), calls=%async_computation.1 | async-start | bytes 688128 | tf_op jit(solution)/shard_map/all_to_all | solution.py:201
Sparse Core Ops, SparseCore 0:
  10.9 112.7 all-gather.1
where the time goes:
time: 516 us; the launch traced here: 511 us
  blocking collectives  187 us (36%)
  matrix products  136 us (26%)
  local copies, waits for them, and re-layouts  123 us (24%)
  other arithmetic  37.6 us (7%)
  between operations  15.2 us (3%)
  starting transfers between devices  6.29 us (1%)
    psum x1, blocking collectives, body(): lax.psum(jnp.sum(grouped, axis=(1, 3), keepdims=True), 'patch') / cell_count  67.8 us
    psum x1, blocking collectives, body(): lax.psum(jnp.sum(centered * centered, axis=(1, 3), keepdims=True), 'patch')  65.5 us
    dot_general x45, matrix products, one_head(): jnp.einsum('fqd,fkd->fqk', query_one, key_one, preferred_element_type=jnp...  65.3 us
    dot_general x45, matrix products, one_head(): jnp.einsum('fqk,fkd->fqd', weights.astype(jnp.bfloat16), value_one, prefe...  53.4 us
    all_gather x1, blocking collectives, body(): factor_piece = lax.all_gather(factor_bf, 'patch', axis=1, tiled=True)  42.3 us
    reshape x19, local copies, waits for them, and re-layouts, split_heads(): values.reshape(frame_count, row_count * column_count, channels // head_si...  37.9 us
    dynamic_slice x40, local copies, waits for them, and re-layouts, fold_heads(): lax.map(one_head, (state_in[0], state_in[1], state_in[2], query_heads, ke...  36.8 us
    while x48, local copies, waits for them, and re-layouts  23 us
  transfers between devices with their start and end apart: 2, of which 1 were waited for; matrix products, arithmetic and copies ran while one was open for 4% of the time, Pallas kernels for 0%

commit v1 on v0

v1 whole, which is shorter than its diff:
```python
import functools
import math

import jax
import jax.numpy as jnp
import numpy as np
from jax import lax
from jax.experimental import pallas as pl
from jax.experimental.pallas import tpu as pltpu
from jax.sharding import PartitionSpec as P

HEAD = 64
HEADS = 5
C = 320
CP = 384
GROUP_WIDTH = 10
FRAMES = 16
ROWS = 64
W = 112
BAND = 224
MINE = 2 * BAND
BOTH = 2 * MINE
ZS = 8
PACK = 560
CHUNK = 32
WORKERS = 14
MESH = pl.DeviceIdType.MESH
F32 = jnp.float32
BF16 = jnp.bfloat16
LOG2E = 1.4426950408889634


def dot(a, b):
    return jnp.dot(a, b, preferred_element_type=F32)


def place():
    f, p = lax.axis_index("frame"), lax.axis_index("patch")
    return f // 4, f % 4, p // 4, (p // 2) % 2, p % 2


def device(x_lo, y, z, x_hi, core):
    return (x_lo * 4 + y, z * 4 + x_hi * 2 + core)


def remote(src, dst, send, recv, target):
    return pltpu.make_async_remote_copy(
        src_ref=src, dst_ref=dst, send_sem=send, recv_sem=recv, device_id=target, device_id_type=MESH
    )


def factor_row(ex_ref, frame, row, inverse):
    lane = lax.broadcasted_iota(jnp.int32, (1, C), 1) // HEAD
    power = jnp.zeros((1, C), jnp.int32)
    for block in range(C // HEAD):
        power = jnp.where(lane == block, ex_ref[frame, row, block], power)
    if inverse:
        power = -power
    out = jnp.full((1, C), 1.0, F32)
    for e in (-2, -1, 1, 2):
        out = jnp.where(power == e, 2.0**e, out)
    return out


def spatial_kernel(
    ts_ref, ex_ref, lat_ref, code_ref, tw_ref, gain_ref, bias_ref, wqkv_ref, wout_ref,
    sec_ref, res_ref,
    lat_in, stage, ring, st_mine, st_twin, st_comb, st_z, st_fin, st_own,
    w01, wlo, whi, wq, woutp, qcomp, qz, kt, vb, kt3, v3, m_ref, acc_ref, msend, mrecv,
    x_send, lat_recv, code_recv, rs_right, rs_left, rr_right, rr_left,
    tw_sems, z_send, z_recv, own_send, own_recv, q_sems, mg_sems,
):
    x_lo, y, z, x_hi, core = place()
    twin = device(x_lo, y, z, x_hi, 1 - core)
    right = device(x_lo, y, (z + 1) % ZS, x_hi, core)
    left = device(x_lo, y, (z + ZS - 1) % ZS, x_hi, core)
    sides = [device(1 - x_lo, y, z, parity, core) for parity in range(2)]
    zpeers = [device(x_lo, y, (z + d) % ZS, x_hi, core) for d in range(1, ZS)]

    barrier = pltpu.get_barrier_semaphore()
    for peer in [twin] + sides + zpeers:
        pl.semaphore_signal(barrier, inc=1, device_id=peer, device_id_type=MESH)
    pl.semaphore_wait(barrier, 3 + ZS - 1)

    def lat_copy(parity, band):
        return remote(lat_ref.at[parity], lat_in.at[band], x_send.at[parity], lat_recv.at[band], sides[parity])

    def code_copy(parity, band):
        return remote(stage.at[parity], ring.at[0, band], x_send.at[2 + parity], code_recv.at[band], sides[parity])

    for parity in range(2):
        lat_copy(parity, x_hi).start()
    for parity in range(2):
        rows = [
            code_ref[parity, r].astype(F32) * factor_row(ex_ref, parity, r, False) for r in range(2)
        ]
        for r in range(2):
            for slab in range(2):
                stage[parity, slab * BAND + r * W : slab * BAND + (r + 1) * W, :] = rows[r][
                    :, slab * 128 : (slab + 1) * 128
                ].astype(BF16)
        stage[parity, 2 * BAND :, :] = jnp.concatenate(
            [rows[0][:, 256:320], rows[1][:, 256:320]], axis=1
        ).astype(BF16)
        code_copy(parity, x_hi).start()

    def to_right(step, band):
        return remote(
            ring.at[step - 1, band], ring.at[step, band],
            rs_right.at[(step - 1) * 2 + band], rr_right.at[(step - 1) * 2 + band], right,
        )

    def to_left(step, band):
        return remote(
            ring.at[jnp.where(step == 1, 0, step + 2), band], ring.at[step + 3, band],
            rs_left.at[(step - 1) * 2 + band], rr_left.at[(step - 1) * 2 + band], left,
        )

    def far_right():
        return remote(ring.at[3, 0], ring.at[7, 0], rs_right.at[6], rr_right.at[6], right)

    def far_left():
        return remote(ring.at[6, 1], ring.at[7, 1], rs_left.at[6], rr_left.at[6], left)

    wq[...] = jnp.concatenate([wqkv_ref[:, :C], jnp.zeros((C, CP - C), BF16)], axis=1)
    pad = jnp.zeros((C, CP - C), BF16)
    wkv = jnp.concatenate([wqkv_ref[:, C : 2 * C], pad, wqkv_ref[:, 2 * C :], pad], axis=1)
    w01[...] = wkv[:256]
    wlo[:64] = wkv[256:]
    wlo[64:] = jnp.zeros((64, 2 * CP), BF16)
    whi[:64] = jnp.zeros((64, 2 * CP), BF16)
    whi[64:] = wkv[256:]
    woutp[:C] = wout_ref[...]
    woutp[C:] = jnp.zeros((CP - C, C), BF16)
    vb[:, CP:] = jnp.ones((BOTH, 128), BF16)
    for i in range(3):
        v3[i, :, CP:] = jnp.ones((MINE, 128), BF16)

    lane = lax.broadcasted_iota(jnp.int32, (1, C), 1)
    half = C // 2
    index = jnp.where(lane < half, lane, lane - half).astype(F32)
    angle = ts_ref[0].astype(F32) * jnp.exp(-math.log(10000.0) * index / half)
    embed = jnp.where(lane < half, jnp.cos(angle), jnp.sin(angle)).astype(BF16)
    shift = dot(jnp.broadcast_to(embed, (16, C)), tw_ref[...])[0:1]

    for band in range(2):
        code_copy(0, band).wait_recv()
        to_right(1, band).start()
        to_left(1, band).start()

    def two_rows(first, second):
        row = lax.broadcasted_iota(jnp.int32, (8, C), 0)
        return jnp.where(row == 0, first, jnp.where(row == 1, second, 0.0))

    for band in range(2):
        lat_copy(0, band).wait_recv()
    wide = lat_in[...].reshape(MINE, C).astype(F32)
    mean = jnp.sum(wide, axis=0, keepdims=True) / MINE
    deviation = wide - mean
    st_mine[...] = two_rows(mean, jnp.sum(deviation * deviation, axis=0, keepdims=True))
    to_twin = remote(st_mine, st_twin, tw_sems.at[0], tw_sems.at[1], twin)
    to_twin.start()
    to_twin.wait_recv()
    delta = st_mine[0:1] - st_twin[0:1]
    st_comb[...] = two_rows(
        (st_mine[0:1] + st_twin[0:1]) * 0.5, st_mine[1:2] + st_twin[1:2] + delta * delta * (MINE / 2)
    )
    z_copies = [remote(st_comb, st_z.at[d], z_send.at[d], z_recv.at[d], zpeers[d - 1]) for d in range(1, ZS)]
    for copy in z_copies:
        copy.start()

    def project(blocks):
        x01 = jnp.concatenate(
            [jnp.concatenate([ring[s, b, :BAND], ring[s, b, BAND : 2 * BAND]], axis=1) for s, b in blocks], axis=0
        )
        tail = jnp.concatenate([ring[s, b, 2 * BAND :] for s, b in blocks], axis=0)
        low, high = dot(tail, wlo[...]), dot(tail, whi[...])
        rest = []
        for i in range(len(blocks)):
            rest += [low[i * W : (i + 1) * W], high[i * W : (i + 1) * W]]
        both = (dot(x01, w01[...]) + jnp.concatenate(rest, axis=0)).astype(BF16)
        return both[:, :CP], both[:, CP:]

    stale_k, stale_v = project([(0, 0), (0, 1)])
    kt3[2] = stale_k.T
    v3[2, :, :CP] = stale_v

    for copy in z_copies:
        copy.wait_recv()
    means = [st_comb[0:1]] + [st_z[d, 0:1] for d in range(1, ZS)]
    total = sum(means[1:], means[0]) / ZS
    squares = st_comb[1:2]
    for d in range(1, ZS):
        squares = squares + st_z[d, 1:2]
    for one in means:
        squares = squares + (one - total) * (one - total) * (2 * MINE)
    g_row = lax.broadcasted_iota(jnp.int32, (C, C), 0) // GROUP_WIDTH
    g_col = lax.broadcasted_iota(jnp.int32, (C, C), 1) // GROUP_WIDTH
    same = (g_row == g_col).astype(F32)

    def group_sum(row):
        return jnp.dot(
            jnp.broadcast_to(row, (8, C)), same, preferred_element_type=F32, precision=lax.Precision.HIGHEST
        )[0:1]

    cells = ROWS * W
    group_mean = group_sum(total) / GROUP_WIDTH
    off = total - group_mean
    group_var = group_sum(squares + off * off * cells) / (cells * GROUP_WIDTH)
    rstd = lax.rsqrt(group_var + 1e-05)
    st_fin[...] = two_rows(group_mean, rstd)
    own_copies = [
        remote(st_fin, st_own.at[x_hi], own_send.at[i], own_recv.at[x_hi], sides[i]) for i in range(2)
    ]
    for copy in own_copies:
        copy.start()

    gain, bias = gain_ref[...], bias_ref[...]
    normed = ((wide - group_mean) * rstd * gain + bias + shift).astype(BF16)
    qcomp[0] = (dot(normed, wq[...]) * (HEAD**-0.5 * LOG2E)).astype(BF16)
    q_copy = remote(qcomp.at[0], qcomp.at[1], q_sems.at[0], q_sems.at[1], twin)
    q_copy.start()
    fresh = (dot(normed[:, :256], w01[...]) + dot(normed[:, 256:], wlo[:64])).astype(BF16)
    fresh_k, fresh_v = fresh[:, :CP], fresh[:, CP:]
    kt3[0] = jnp.concatenate([fresh_k[:BAND], stale_k[BAND:]], axis=0).T
    kt3[1] = jnp.concatenate([stale_k[:BAND], fresh_k[BAND:]], axis=0).T
    v3[0, :BAND, :CP] = fresh_v[:BAND]
    v3[0, BAND:, :CP] = stale_v[BAND:]
    v3[1, :BAND, :CP] = stale_v[:BAND]
    v3[1, BAND:, :CP] = fresh_v[BAND:]

    m_ref[...] = jnp.full(m_ref.shape, -1e30, F32)
    acc_ref[...] = jnp.zeros(acc_ref.shape, F32)
    lane128 = lax.broadcasted_iota(jnp.int32, (1, 128), 1)
    low_half = lane128 < HEAD

    def pass_on(step):
        for band in range(2):
            to_right(step, band).wait_recv()
            to_right(step + 1, band).start()
            to_left(step, band).wait_recv()
            to_left(step + 1, band).start()

    pass_on(1)
    q_copy.wait_recv()
    for who in range(2):
        for h in range(HEADS):
            slab = qcomp[who, :, (h // 2) * 128 : (h // 2) * 128 + 128]
            keep = low_half if h % 2 == 0 else jnp.logical_not(low_half)
            qz[h, who * MINE : (who + 1) * MINE, :] = jnp.where(keep, slab, jnp.zeros_like(slab))

    def attend(scores_of, values_of):
        scores = scores_of(0)
        for h in range(HEADS):
            following = scores_of(h + 1) if h < HEADS - 1 else None
            old = m_ref[h][:, :1]
            peak = jnp.maximum(old, jnp.max(scores, axis=1, keepdims=True))
            weights = jnp.exp2(scores - peak).astype(BF16)
            m_ref[h] = jnp.broadcast_to(peak, (BOTH, 128))
            acc_ref[h] = acc_ref[h] * jnp.exp2(old - peak) + values_of(h, weights)
            scores = following

    parts = ((0, 0, BAND), (1, BAND, MINE), (2, MINE, BOTH))

    def own_scores(h):
        s = h // 2 * 128
        return jnp.concatenate([dot(qz[h, a:b], kt3[i, s : s + 128]) for i, a, b in parts], axis=0)

    def own_values(h, weights):
        s = h // 2 * 128
        return jnp.concatenate(
            [
                dot(weights[a:b], jnp.concatenate([v3[i, :, s : s + 128], v3[i, :, CP:]], axis=1))
                for i, a, b in parts
            ],
            axis=0,
        )

    attend(own_scores, own_values)

    def block(blocks):
        keys = len(blocks) * BAND
        k, v = project(blocks)
        kt[:, :keys] = k.T
        vb[:keys, :CP] = v

        def scores_of(h):
            s = h // 2 * 128
            return dot(qz[h], kt[s : s + 128, :keys])

        def values_of(h, weights):
            s = h // 2 * 128
            return dot(weights, jnp.concatenate([vb[:keys, s : s + 128], vb[:keys, CP:]], axis=1))

        attend(scores_of, values_of)

    def ring_turn(i, carry):
        @pl.when(i == 1)
        def _():
            pass_on(2)

        @pl.when(i == 2)
        def _():
            for band in range(2):
                to_right(3, band).wait_recv()
                to_left(3, band).wait_recv()
            far_right().start()
            far_left().start()

        block([(i, 0), (i, 1), (i + 3, 0), (i + 3, 1)])
        return carry

    lax.fori_loop(1, 4, ring_turn, 0)
    far_right().wait_recv()
    far_left().wait_recv()
    block([(7, 0), (7, 1)])

    stats = jnp.zeros((MINE, 128), F32)
    for h in range(HEADS):
        stats = jnp.where(lane128 == h, m_ref[h, MINE:], stats)
        stats = jnp.where(lane128 == 8 + h, acc_ref[h, MINE:, 128:], stats)
    for slab in range(3):
        one = acc_ref[2 * slab, MINE:, :128]
        if slab < 2:
            one = jnp.where(low_half, one, acc_ref[2 * slab + 1, MINE:, :128])
        msend[:, slab * 128 : (slab + 1) * 128] = one
    msend[:, CP:] = stats
    merge = remote(msend, mrecv, mg_sems.at[0], mg_sems.at[1], twin)
    merge.start()

    for parity in range(2):
        remote(st_fin, st_own.at[parity], own_send.at[0], own_recv.at[parity], sides[0]).wait_recv()
        for r in range(2):
            own = lat_ref[parity, r].astype(F32)
            normed_own = ((own - st_own[parity, 0:1]) * st_own[parity, 1:2] * gain + bias + shift).astype(BF16)
            stale_own = code_ref[parity, r].astype(F32) * factor_row(ex_ref, parity, r, False)
            res_ref[parity, r] = (
                (normed_own.astype(F32) - stale_own) * factor_row(ex_ref, parity, r, True)
            ).astype(BF16)

    merge.wait_recv()
    keep_own, keep_other, sums = [], [], []
    for h in range(HEADS):
        mine, other = m_ref[h, :MINE], mrecv[:, CP + h : CP + h + 1]
        peak = jnp.maximum(mine, other)
        a, b = jnp.exp2(mine - peak), jnp.exp2(other - peak)
        keep_own.append(a)
        keep_other.append(b)
        sums.append(acc_ref[h, :MINE, 128:] * a + mrecv[:, CP + 8 + h : CP + 9 + h] * b)
    slabs = []
    for slab in range(3):
        e, o = 2 * slab, min(2 * slab + 1, HEADS - 1)

        def pick(values):
            return values[e] if e == o else jnp.where(low_half, values[e], values[o])

        own_sum = pick([acc_ref[h, :MINE, :128] for h in range(HEADS)])
        joined = own_sum * pick(keep_own) + mrecv[:, slab * 128 : (slab + 1) * 128] * pick(keep_other)
        slabs.append((joined / pick(sums)).astype(BF16))
    attended = jnp.concatenate(slabs, axis=1)
    sec_ref[...] = (wide_again(lat_in) + dot(attended, woutp[...])).astype(BF16)

    for parity in range(2):
        lat_copy(parity, x_hi).wait_send()
        code_copy(parity, x_hi).wait_send()
    to_twin.wait_send()
    for copy in z_copies + own_copies:
        copy.wait_send()
    q_copy.wait_send()
    merge.wait_send()
    for step in range(1, 4):
        for band in range(2):
            to_right(step, band).wait_send()
            to_left(step, band).wait_send()
    far_right().wait_send()
    far_left().wait_send()


def wide_again(lat_in):
    return lat_in[...].reshape(MINE, C).astype(F32)


def worker_place(j):
    owner = j // 2
    return 1 - owner // 4, owner % 4, j % 2


def temporal_kernel(
    sec_ref, embed_ref, wqkv_ref, wout_ref, out_ref,
    xin, yout, wp, woutp, f_send, f_recv, b_send, b_recv, local_sem,
):
    x_lo, y, z, x_hi, core = place()
    frame = 2 * ((1 - x_lo) * 4 + y) + x_hi

    barrier = pltpu.get_barrier_semaphore()
    places = [worker_place(j) for j in range(FRAMES)]
    devices = [device(a, b, z, c, core) for a, b, c in places]
    for j in range(FRAMES):

        @pl.when(frame != j)
        def _():
            pl.semaphore_signal(barrier, inc=1, device_id=devices[j], device_id_type=MESH)

    pl.semaphore_wait(barrier, FRAMES - 1)

    def forward(j, source):
        return remote(
            sec_ref.at[pl.ds(j * CHUNK, CHUNK)], xin.at[source], f_send.at[j], f_recv.at[source], devices[j]
        )

    for j in range(WORKERS):

        @pl.when(frame != j)
        def _():
            forward(j, frame).start()

        @pl.when(frame == j)
        def _():
            pltpu.make_async_copy(sec_ref.at[pl.ds(j * CHUNK, CHUNK)], xin.at[j], local_sem.at[0]).start()

    pad = jnp.zeros((C, CP - C), BF16)
    wp[...] = jnp.concatenate(
        [wqkv_ref[:, :C], pad, wqkv_ref[:, C : 2 * C], pad, wqkv_ref[:, 2 * C :], pad], axis=1
    )
    woutp[:C] = wout_ref[...]
    woutp[C:] = jnp.zeros((CP - C, C), BF16)

    band = frame // 7
    spot = frame % 7

    def back(target):
        return remote(
            yout.at[pl.ds(2 * target, 2)],
            out_ref.at[pl.ds(0, 2), pl.ds(spot * CHUNK, CHUNK)],
            b_send.at[target],
            b_recv.at[spot],
            device(target // 4, target % 4, z, band, core),
        )

    def back_local(target):
        return pltpu.make_async_copy(
            yout.at[pl.ds(2 * target, 2)],
            out_ref.at[pl.ds(0, 2), pl.ds(spot * CHUNK, CHUNK)],
            local_sem.at[1],
        )

    here = x_lo * 4 + y

    @pl.when(frame < WORKERS)
    def _():
        for j in range(FRAMES):

            @pl.when(frame != j)
            def _():
                forward(0, j).wait_recv()

            @pl.when(frame == j)
            def _():
                pltpu.make_async_copy(sec_ref.at[pl.ds(0, CHUNK)], xin.at[j], local_sem.at[0]).wait()

        low_half = lax.broadcasted_iota(jnp.int32, (1, 128), 1) < HEAD
        tile = FRAMES * 16
        row_cell = lax.broadcasted_iota(jnp.int32, (tile, tile), 0) % 16
        col_cell = lax.broadcasted_iota(jnp.int32, (tile, tile), 1) % 16
        same = row_cell == col_cell
        for part in range(CHUNK // 16):
            section = xin[:, part * 16 : (part + 1) * 16, :].astype(F32)
            shifted = (section + embed_ref[...][:, None, :]).reshape(tile, C)
            mean = jnp.mean(shifted, axis=-1, keepdims=True)
            deviation = shifted - mean
            normed = (
                deviation * lax.rsqrt(jnp.mean(deviation * deviation, axis=-1, keepdims=True) + 1e-05)
            ).astype(BF16)
            proj = dot(normed, wp[...]).astype(BF16)
            mixed = []
            for slab in range(3):
                q = proj[:, slab * 128 : (slab + 1) * 128]
                k = proj[:, CP + slab * 128 : CP + (slab + 1) * 128]
                v = proj[:, 2 * CP + slab * 128 : 2 * CP + (slab + 1) * 128]
                halves = []
                for h in range(2 if slab < 2 else 1):
                    keep = low_half if h == 0 else jnp.logical_not(low_half)
                    scores = lax.dot_general(
                        jnp.where(keep, q, jnp.zeros_like(q)), k, (((1,), (1,)), ((), ())),
                        preferred_element_type=F32,
                    ) * (HEAD**-0.5)
                    scores = jnp.where(same, scores, -1e30)
                    weights = jnp.exp(scores - jnp.max(scores, axis=1, keepdims=True))
                    below = jnp.sum(weights, axis=1, keepdims=True)
                    halves.append(dot(weights.astype(BF16), v) / below)
                mixed.append(halves[0] if slab == 2 else jnp.where(low_half, halves[0], halves[1]))
            mix = jnp.concatenate(mixed, axis=1).astype(BF16)
            result = section.reshape(tile, C) + dot(mix, woutp[...])
            yout[:, part * 16 : (part + 1) * 16, :] = result.astype(BF16).reshape(FRAMES, 16, C)
        for target in range(8):
            stays = jnp.logical_and(here == target, x_hi == band)

            @pl.when(stays)
            def _():
                back_local(target).start()

            @pl.when(jnp.logical_not(stays))
            def _():
                back(target).start()

    for s in range(7):
        source = x_hi * 7 + s

        @pl.when(frame == source)
        def _():
            pltpu.make_async_copy(
                yout.at[pl.ds(0, 2)], out_ref.at[pl.ds(0, 2), pl.ds(s * CHUNK, CHUNK)], local_sem.at[1]
            ).wait()

        @pl.when(frame != source)
        def _():
            remote(
                yout.at[pl.ds(0, 2)], out_ref.at[pl.ds(0, 2), pl.ds(s * CHUNK, CHUNK)],
                b_send.at[0], b_recv.at[s], devices[0],
            ).wait_recv()

    for j in range(WORKERS):

        @pl.when(frame != j)
        def _():
            forward(j, frame).wait_send()

    @pl.when(frame < WORKERS)
    def _():
        for target in range(8):

            @pl.when(jnp.logical_not(jnp.logical_and(here == target, x_hi == band)))
            def _():
                back(target).wait_send()


def frame_table():
    half = C // 2
    frequency = np.exp(-math.log(10000.0) * np.arange(half) / half)
    angles = np.arange(FRAMES)[:, None] * frequency
    return np.concatenate([np.cos(angles), np.sin(angles)], axis=-1).astype(np.float32)


VM = pl.BlockSpec(memory_space=pltpu.VMEM)
SM = pl.BlockSpec(memory_space=pltpu.SMEM)


def body(
    latent, timestep, time_weight, norm_gain, norm_bias, spatial_qkv, spatial_out,
    stale_codes, stale_exponents, temporal_qkv, temporal_out,
):
    dma = pltpu.SemaphoreType.DMA
    section, residual = pl.pallas_call(
        spatial_kernel,
        out_shape=(
            jax.ShapeDtypeStruct((MINE, C), BF16),
            jax.ShapeDtypeStruct((2, 2, W, C), BF16),
        ),
        in_specs=[SM, SM] + [VM] * 7,
        out_specs=(VM, VM),
        scratch_shapes=[
            pltpu.VMEM((2, 2, W, C), BF16),
            pltpu.VMEM((2, PACK, 128), BF16),
            pltpu.VMEM((ZS, 2, PACK, 128), BF16),
            pltpu.VMEM((8, C), F32),
            pltpu.VMEM((8, C), F32),
            pltpu.VMEM((8, C), F32),
            pltpu.VMEM((ZS, 8, C), F32),
            pltpu.VMEM((8, C), F32),
            pltpu.VMEM((2, 8, C), F32),
            pltpu.VMEM((256, 2 * CP), BF16),
            pltpu.VMEM((128, 2 * CP), BF16),
            pltpu.VMEM((128, 2 * CP), BF16),
            pltpu.VMEM((C, CP), BF16),
            pltpu.VMEM((CP, C), BF16),
            pltpu.VMEM((2, MINE, CP), BF16),
            pltpu.VMEM((HEADS, BOTH, 128), BF16),
            pltpu.VMEM((CP, BOTH), BF16),
            pltpu.VMEM((BOTH, 512), BF16),
            pltpu.VMEM((3, CP, MINE), BF16),
            pltpu.VMEM((3, MINE, 512), BF16),
            pltpu.VMEM((HEADS, BOTH, 128), F32),
            pltpu.VMEM((HEADS, BOTH, 256), F32),
            pltpu.VMEM((MINE, 512), F32),
            pltpu.VMEM((MINE, 512), F32),
            dma((4,)), dma((2,)), dma((2,)), dma((7,)), dma((7,)), dma((7,)), dma((7,)),
            dma((2,)), dma((ZS,)), dma((ZS,)), dma((2,)), dma((2,)), dma((2,)), dma((2,)),
        ],
        compiler_params=pltpu.CompilerParams(
            collective_id=0, has_side_effects=True, vmem_limit_bytes=60 * 2**20
        ),
        name="spatial",
    )(
        timestep, stale_exponents, latent, stale_codes, time_weight,
        norm_gain.reshape(1, C), norm_bias.reshape(1, C), spatial_qkv, spatial_out,
    )
    output = pl.pallas_call(
        temporal_kernel,
        out_shape=jax.ShapeDtypeStruct((2, BAND, C), BF16),
        in_specs=[VM] * 4,
        out_specs=VM,
        scratch_shapes=[
            pltpu.VMEM((FRAMES, CHUNK, C), BF16),
            pltpu.VMEM((FRAMES, CHUNK, C), BF16),
            pltpu.VMEM((C, 3 * CP), BF16),
            pltpu.VMEM((CP, C), BF16),
            dma((WORKERS,)), dma((FRAMES,)), dma((8,)), dma((7,)), dma((2,)),
        ],
        compiler_params=pltpu.CompilerParams(
            collective_id=1, has_side_effects=True, vmem_limit_bytes=40 * 2**20
        ),
        name="temporal",
    )(section, jnp.asarray(frame_table()), temporal_qkv, temporal_out)
    return output.reshape(2, 2, W, C), residual


def solution(mesh):
    placed = (
        P("frame", "patch", None, None),
        P(),
        P(),
        P(),
        P(),
        P(),
        P(),
        P("frame", "patch", None, None),
        P("frame", "patch", None),
        P(),
        P(),
    )
    return jax.shard_map(
        body,
        mesh=mesh,
        in_specs=placed,
        out_specs=(P("frame", "patch", None, None), P("frame", "patch", None, None)),
        check_vma=False,
    )
```

time: 516 us -> 102 us (0.20)
  blocking collectives: 187 us -> 0 us
  matrix products: 136 us -> 0 us
  local copies, waits for them, and re-layouts: 123 us -> 7.5 us
  Pallas kernels: 0 us -> 92.3 us
  other arithmetic: 37.6 us -> 0 us
  between operations: 15.2 us -> 1.35 us
  starting transfers between devices: 6.29 us -> 0 us
    dot_general x105 -> x0, matrix products: 136 us -> none  [the longest x45 65.3 us: one_head(): jnp.einsum('fqd,fkd->fqk', query_one, key_one, preferred_element_type=jnp...]
    psum x2 -> x0, blocking collectives: 133 us -> none  [the longest x1 67.8 us: body(): lax.psum(jnp.sum(grouped, axis=(1, 3), keepdims=True), 'patch') / cell_count]
    pallas_call x0 -> x2, Pallas kernels: none -> 92.3 us  [the longest x1 71 us: body(): pl.pallas_call(spatial_kernel, out_shape=(jax.ShapeDtypeStruct((MINE, C),...]
    reshape x63 -> x2, local copies, waits for them, and re-layouts: 46.2 us -> 1.81 us  [the longest x1 1.25 us: body(): norm_gain.reshape(1, C)]
    all_gather x1 -> x0, blocking collectives: 42.3 us -> none  [body(): factor_piece = lax.all_gather(factor_bf, 'patch', axis=1, tiled=True)]
    dynamic_slice x48 -> x0, local copies, waits for them, and re-layouts: 36.9 us -> none  [the longest x40 36.8 us: fold_heads(): lax.map(one_head, (state_in[0], state_in[1], state_in[2], query_heads, ke...]
    while x49 -> x0, local copies, waits for them, and re-layouts: 23.7 us -> none
    reduce_sum x52 -> x0, other arithmetic: 19.7 us -> none  [the longest x45 17.3 us: one_head(): new_totals = head_totals * keep_share + jnp.sum(weights, axis=-1)]
  transfers between devices with their start and end apart: 2 -> 0, of which waited for: 1 -> 0; matrix products, arithmetic and copies ran while one was open for 4% -> 0% of each run, Pallas kernels for 0% -> 0%
where the time goes in v1:
time: 102 us; the launch traced here: 101 us
  Pallas kernels  92.3 us (90%)
  local copies, waits for them, and re-layouts  7.5 us (7%)
  between operations  1.35 us (1%)
    pallas_call x1, Pallas kernels, body(): pl.pallas_call(spatial_kernel, out_shape=(jax.ShapeDtypeStruct((MINE, C),...  71 us
    pallas_call x1, Pallas kernels, body(): pl.pallas_call(temporal_kernel, out_shape=jax.ShapeDtypeStruct((2, BAND,...  21.4 us
    unnamed x18, local copies, waits for them, and re-layouts  5.69 us

profile of v1, /device:TPU:30, one launch (start us, length us, event | category | flops | bytes accessed | tf_op | source)
XLA Modules:
  0.0 101.2 jit_solution(7564189214619546261)
XLA Ops:
  1.3 0.0 copy-start.6
  1.3 1.3 %reshape.13.gain_ref = f32[1,320]{1,0:T(1,128)} reshape(f32[320]{0:T(512)} %param.15) | data formatting | bytes 2560 | tf_op jit(solution)/shard_map/reshape | solution.py:595
  2.5 0.0 copy-done.6
  2.5 0.6 reshape.14.bias_ref
  3.1 0.0 copy-start.5
  3.1 1.9 %copy.14.lat_ref = bf16[2,2,112,320]{3,2,1,0:T(8,128)(2,1)} copy(bf16[2,2,112,320]{2,3,1,0:T(8,128)(2,1)} %param.12) | data formatting | bytes 573440 | tf_op args[0]
  5.0 0.0 copy-done.5
  5.0 0.9 copy.15.code_ref
  5.9 0.0 copy-start
  5.9 0.0 copy-start.2
  5.9 0.0 copy-start.3
  5.9 71.0 %spatial.1 = (bf16[448,320]{1,0:T(8,128)(2,1)}, bf16[2,2,112,320]{3,2,1,0:T(8,128)(2,1)}) custom-call(s32[1]{0:T(128)S(6)} %copy.18.ts_ref, s32[2,2,5]{2,1,0:T(2,128)} %ex_ref.1, bf16[2,2,112,320]{3,2,1,0:T(8,128)(2,1)} %copy.14.lat_ref, bf16[2,2,112,320]{3,2,1,0:T(8,128)(2,1)} %copy.15.code_ref, bf16[320,320]{1,0:T(8,128)(2,1)} %tw_ref.1, ...), custom_call_target="tpu_custom_call" | custom-call | tf_op jit(solution)/shard_map/spatial/pallas_call | solution.py:553
  76.9 0.0 copy-done
  76.9 0.0 copy-done.2
  76.9 0.0 copy-done.3
  76.9 0.0 copy-start.1
  77.0 1.0 copy-done.1
  77.9 21.4 %temporal.1 = bf16[2,224,320]{2,1,0:T(8,128)(2,1)S(1)} custom-call(bf16[448,320]{1,0:T(8,128)(2,1)S(1)} %copy-done.1, f32[16,320]{1,0:T(8,128)S(1)} %copy-done.3, bf16[320,960]{1,0:T(8,128)(2,1)S(1)} %copy-done, bf16[320,320]{1,0:T(8,128)(2,1)S(1)} %copy-done.2), custom_call_target="tpu_custom_call" | custom-call | tf_op jit(solution)/shard_map/temporal/pallas_call | solution.py:597
  99.3 0.0 copy-start.4
  99.3 0.9 copy.16
  100.2 0.1 copy-done.4
  100.3 0.9 copy.17
Async XLA Ops:
  1.3 1.3 %copy-start.6 = (f32[320]{0:T(512)S(1)}, f32[320]{0:T(512)}, u32[]{:S(2)}) copy-start(f32[320]{0:T(512)} %param.16) | copy-start | bytes 3844
  3.1 1.9 %copy-start.5 = (bf16[2,2,112,320]{2,3,1,0:T(8,128)(2,1)S(1)}, bf16[2,2,112,320]{2,3,1,0:T(8,128)(2,1)}, u32[]{:S(2)}) copy-start(bf16[2,2,112,320]{2,3,1,0:T(8,128)(2,1)} %param.19) | copy-start | bytes 860164
  5.9 71.0 %copy-start = (bf16[320,960]{1,0:T(8,128)(2,1)S(1)}, bf16[320,960]{1,0:T(8,128)(2,1)}, u32[]{:S(2)}) copy-start(bf16[320,960]{1,0:T(8,128)(2,1)} %wqkv_ref.3) | copy-start | bytes 1843204
  5.9 71.0 %copy-start.2 = (bf16[320,320]{1,0:T(8,128)(2,1)S(1)}, bf16[320,320]{1,0:T(8,128)(2,1)}, u32[]{:S(2)}) copy-start(bf16[320,320]{1,0:T(8,128)(2,1)} %wout_ref.3) | copy-start | bytes 614404
  5.9 71.0 %copy-start.3 = (f32[16,320]{1,0:T(8,128)S(1)}, f32[16,320]{1,0:T(8,128)}, u32[]{:S(2)}) copy-start(f32[16,320]{1,0:T(8,128)} %constant.2.clone.embed_ref) | copy-start | bytes 61444
  76.9 1.0 copy-start.1
  99.3 1.0 copy-start.4

commit v2 on v1

v2 whole, which is shorter than its diff:
```python
import functools
import math

import jax
import jax.numpy as jnp
import numpy as np
from jax import lax
from jax.experimental import pallas as pl
from jax.experimental.pallas import tpu as pltpu
from jax.sharding import PartitionSpec as P

HEAD = 64
HEADS = 5
C = 320
CP = 384
GROUP_WIDTH = 10
FRAMES = 16
ROWS = 64
W = 112
BAND = 224
MINE = 2 * BAND
BOTH = 2 * MINE
ZS = 8
PACK = 560
CELLS = 32
WORKERS = 14
KEYS = 8 * BAND
FIRST = 512
MESH = pl.DeviceIdType.MESH
F32 = jnp.float32
BF16 = jnp.bfloat16
LOG2E = 1.4426950408889634


def dot(a, b):
    return jnp.dot(a, b, preferred_element_type=F32)


def place():
    f, p = lax.axis_index("frame"), lax.axis_index("patch")
    return f // 4, f % 4, p // 4, (p // 2) % 2, p % 2


def device(x_lo, y, z, x_hi, core):
    return (x_lo * 4 + y, z * 4 + x_hi * 2 + core)


def remote(src, dst, send, recv, target):
    return pltpu.make_async_remote_copy(
        src_ref=src, dst_ref=dst, send_sem=send, recv_sem=recv, device_id=target, device_id_type=MESH
    )


def factor_row(ex_ref, frame, row):
    lane = lax.broadcasted_iota(jnp.int32, (1, C), 1) // HEAD
    power = jnp.zeros((1, C), jnp.int32)
    for block in range(C // HEAD):
        power = jnp.where(lane == block, ex_ref[frame, row, block], power)
    out = jnp.full((1, C), 1.0, F32)
    for e in (-1, 1, 2):
        out = jnp.where(power == e, 2.0**e, out)
    return out


def rows_of(*parts):
    row = lax.broadcasted_iota(jnp.int32, (8, C), 0)
    out = jnp.zeros((8, C), F32)
    for i, part in enumerate(parts):
        out = jnp.where(row == i, part, out)
    return out


def worker_device(j, z, core):
    owner = j // 2
    return device(1 - owner // 4, owner % 4, z, j % 2, core)


def kernel(
    ts_ref, ex_ref, lat_ref, code_ref, tw_ref, gain_ref, bias_ref, wqkv_ref, wout_ref, embed_ref,
    wt_ref, wtout_ref,
    out_ref, res_ref,
    lat_in, wide_ref, stage, ring, st_mine, st_twin, st_comb, st_z, st_side, st_x, st_fin, st_own,
    w01, wlo, whi, wq, woutp, wp, wtoutp, qcomp, qz, kb, kt, vb, kt3, v3, m_ref, acc_ref, msend, mrecv,
    sec, xin, yout, got,
    x_send, lat_recv, code_recv, rs_right, rs_left, rr_right, rr_left,
    tw_sems, z_send, z_recv, sx_send, sx_recv, own_send, own_recv, q_sems, mg_sems,
    f_send, f_recv, b_send, b_recv, local_sem,
):
    x_lo, y, z, x_hi, core = place()
    frame = 2 * ((1 - x_lo) * 4 + y) + x_hi
    twin = device(x_lo, y, z, x_hi, 1 - core)
    right = device(x_lo, y, (z + 1) % ZS, x_hi, core)
    left = device(x_lo, y, (z + ZS - 1) % ZS, x_hi, core)
    sides = [device(1 - x_lo, y, z, parity, core) for parity in range(2)]
    zpeers = [device(x_lo, y, (z + d) % ZS, x_hi, core) for d in range(1, ZS)]

    barrier = pltpu.get_barrier_semaphore()
    plane = [worker_device((frame + k) % FRAMES, z, core) for k in range(1, FRAMES)]
    for peer in [twin] + zpeers + plane:
        pl.semaphore_signal(barrier, inc=1, device_id=peer, device_id_type=MESH)
    pl.semaphore_wait(barrier, 1 + ZS - 1 + FRAMES - 1)

    def lat_copy(parity, band):
        return remote(lat_ref.at[parity], lat_in.at[band], x_send.at[parity], lat_recv.at[band], sides[parity])

    def code_copy(parity, band):
        return remote(stage.at[parity], ring.at[0, band], x_send.at[2 + parity], code_recv.at[band], sides[parity])

    for parity in range(2):
        rows = [
            code_ref[parity, r].astype(F32).T * factor_row(ex_ref, parity, r) for r in range(2)
        ]
        for r in range(2):
            for slab in range(2):
                stage[parity, slab * BAND + r * W : slab * BAND + (r + 1) * W, :] = rows[r][
                    :, slab * 128 : (slab + 1) * 128
                ].astype(BF16)
        stage[parity, 2 * BAND :, :] = jnp.concatenate(
            [rows[0][:, 256:320], rows[1][:, 256:320]], axis=1
        ).astype(BF16)
        code_copy(parity, x_hi).start()
    for parity in range(2):
        lat_copy(parity, x_hi).start()

    stats = []
    for parity in range(2):
        own = jnp.concatenate([lat_ref[parity, r].astype(F32).T for r in range(2)], axis=0)
        mean = jnp.sum(own, axis=0, keepdims=True) / BAND
        deviation = own - mean
        stats += [mean, jnp.sum(deviation * deviation, axis=0, keepdims=True)]
    st_mine[...] = rows_of(*stats)
    to_twin = remote(st_mine, st_twin, tw_sems.at[0], tw_sems.at[1], twin)
    to_twin.start()

    def to_right(step, band):
        return remote(
            ring.at[step - 1, band], ring.at[step, band],
            rs_right.at[(step - 1) * 2 + band], rr_right.at[(step - 1) * 2 + band], right,
        )

    def to_left(step, band):
        return remote(
            ring.at[0 if step == 1 else step + 2, band], ring.at[step + 3, band],
            rs_left.at[(step - 1) * 2 + band], rr_left.at[(step - 1) * 2 + band], left,
        )

    def far_right():
        return remote(ring.at[3, 0], ring.at[7, 0], rs_right.at[6], rr_right.at[6], right)

    def far_left():
        return remote(ring.at[6, 1], ring.at[7, 1], rs_left.at[6], rr_left.at[6], left)

    pad = jnp.zeros((C, CP - C), BF16)
    wq[...] = jnp.concatenate([wqkv_ref[:, :C], pad], axis=1)
    wkv = jnp.concatenate([wqkv_ref[:, C : 2 * C], pad, wqkv_ref[:, 2 * C :], pad], axis=1)
    w01[...] = wkv[:256]
    wlo[:64] = wkv[256:]
    wlo[64:] = jnp.zeros((64, 2 * CP), BF16)
    whi[:64] = jnp.zeros((64, 2 * CP), BF16)
    whi[64:] = wkv[256:]

    to_twin.wait_recv()
    combined = []
    for parity in range(2):
        i = 2 * parity
        delta = st_mine[i : i + 1] - st_twin[i : i + 1]
        combined += [
            (st_mine[i : i + 1] + st_twin[i : i + 1]) * 0.5,
            st_mine[i + 1 : i + 2] + st_twin[i + 1 : i + 2] + delta * delta * (BAND / 2),
        ]
    st_comb[...] = rows_of(*combined)
    z_copies = [remote(st_comb, st_z.at[d], z_send.at[d], z_recv.at[d], zpeers[d - 1]) for d in range(1, ZS)]
    for copy in z_copies:
        copy.start()

    woutp[:C] = wout_ref[...]
    woutp[C:] = jnp.zeros((CP - C, C), BF16)
    wp[...] = jnp.concatenate([wt_ref[:, :C], pad, wt_ref[:, C : 2 * C], pad, wt_ref[:, 2 * C :], pad], axis=1)
    wtoutp[:C] = wtout_ref[...]
    wtoutp[C:] = jnp.zeros((CP - C, C), BF16)
    vb[:, CP:] = jnp.ones((KEYS, 128), BF16)
    for i in range(3):
        v3[i, :, CP:] = jnp.ones((FIRST, 128), BF16)

    lane = lax.broadcasted_iota(jnp.int32, (1, C), 1)
    half = C // 2
    index = jnp.where(lane < half, lane, lane - half).astype(F32)
    angle = ts_ref[0].astype(F32) * jnp.exp(-math.log(10000.0) * index / half)
    embed = jnp.where(lane < half, jnp.cos(angle), jnp.sin(angle)).astype(BF16)
    shift = dot(jnp.broadcast_to(embed, (16, C)), tw_ref[...])[0:1]
    gain = gain_ref[...].reshape(1, C)
    bias = bias_ref[...].reshape(1, C)

    for copy in z_copies:
        copy.wait_recv()
    side_copies = []
    for parity in range(2):
        i = 2 * parity
        means = [st_comb[i : i + 1]] + [st_z[d, i : i + 1] for d in range(1, ZS)]
        total = sum(means[1:], means[0]) / ZS
        squares = st_comb[i + 1 : i + 2]
        for d in range(1, ZS):
            squares = squares + st_z[d, i + 1 : i + 2]
        for one in means:
            squares = squares + (one - total) * (one - total) * (2 * BAND)
        st_side[parity] = rows_of(total, squares)
        copy = remote(st_side.at[parity], st_x.at[x_hi], sx_send.at[parity], sx_recv.at[x_hi], sides[parity])
        copy.start()
        side_copies.append(copy)

    code_copy(0, 0).wait_recv()
    to_right(1, 0).start()
    code_copy(0, 1).wait_recv()
    to_left(1, 1).start()
    to_right(1, 1).start()
    to_left(1, 0).start()

    def project(blocks):
        x01 = jnp.concatenate(
            [jnp.concatenate([ring[s, b, :BAND], ring[s, b, BAND : 2 * BAND]], axis=1) for s, b in blocks], axis=0
        )
        tail = jnp.concatenate([ring[s, b, 2 * BAND :] for s, b in blocks], axis=0)
        low, high = dot(tail, wlo[...]), dot(tail, whi[...])
        rest = []
        for i in range(len(blocks)):
            rest += [low[i * W : (i + 1) * W], high[i * W : (i + 1) * W]]
        both = (dot(x01, w01[...]) + jnp.concatenate(rest, axis=0)).astype(BF16)
        return both[:, :CP], both[:, CP:]

    stale_k, stale_v = project([(0, 0), (0, 1)])

    for band in range(2):
        remote(
            st_side.at[0], st_x.at[band], sx_send.at[0], sx_recv.at[band], sides[0]
        ).wait_recv()
    total = (st_x[0, 0:1] + st_x[1, 0:1]) * 0.5
    delta = st_x[0, 0:1] - st_x[1, 0:1]
    cells = ROWS * W
    squares = st_x[0, 1:2] + st_x[1, 1:2] + delta * delta * (cells / 4)
    g_row = lax.broadcasted_iota(jnp.int32, (C, C), 0) // GROUP_WIDTH
    g_col = lax.broadcasted_iota(jnp.int32, (C, C), 1) // GROUP_WIDTH
    same_group = (g_row == g_col).astype(F32)

    def group_sum(row):
        return jnp.dot(
            jnp.broadcast_to(row, (8, C)), same_group, preferred_element_type=F32, precision=lax.Precision.HIGHEST
        )[0:1]

    group_mean = group_sum(total) / GROUP_WIDTH
    off = total - group_mean
    group_var = group_sum(squares + off * off * cells) / (cells * GROUP_WIDTH)
    rstd = lax.rsqrt(group_var + 1e-05)
    st_fin[...] = rows_of(group_mean, rstd)
    own_copies = [
        remote(st_fin, st_own.at[x_hi], own_send.at[i], own_recv.at[x_hi], sides[i]) for i in range(2)
    ]
    for copy in own_copies:
        copy.start()

    for band in range(2):
        lat_copy(0, band).wait_recv()
        for r in range(2):
            wide_ref[band * BAND + r * W : band * BAND + (r + 1) * W] = (
                lat_in[band, r].astype(F32).T.astype(BF16)
            )
    wide = wide_ref[...].astype(F32)
    normed = ((wide - group_mean) * rstd * gain + bias + shift).astype(BF16)
    qcomp[0] = (dot(normed, wq[...]) * (HEAD**-0.5 * LOG2E)).astype(BF16)
    q_copy = remote(qcomp.at[0], qcomp.at[1], q_sems.at[0], q_sems.at[1], twin)
    q_copy.start()
    fresh = (dot(normed[:, :256], w01[...]) + dot(normed[:, 256:], wlo[:64])).astype(BF16)
    fresh_k, fresh_v = fresh[:, :CP], fresh[:, CP:]

    def pass_right(step, band):
        to_right(step, band).wait_recv()
        to_right(step + 1, band).start()

    def pass_left(step, band):
        to_left(step, band).wait_recv()
        to_left(step + 1, band).start()

    pass_right(1, 0)
    pass_left(1, 1)
    pass_right(1, 1)
    pass_left(1, 0)
    first_k, first_v = project([(1, 0), (1, 1), (4, 0), (4, 1)])
    pass_right(2, 0)
    pass_left(2, 1)
    second_k, second_v = project([(2, 0), (5, 1)])
    lead = FIRST - MINE
    own_k = [
        jnp.concatenate([fresh_k[:BAND], stale_k[BAND:], first_k[:lead]], axis=0),
        jnp.concatenate([stale_k[:BAND], fresh_k[BAND:], first_k[:lead]], axis=0),
        jnp.concatenate([stale_k, first_k[:lead]], axis=0),
    ]
    own_v = [
        jnp.concatenate([fresh_v[:BAND], stale_v[BAND:], first_v[:lead]], axis=0),
        jnp.concatenate([stale_v[:BAND], fresh_v[BAND:], first_v[:lead]], axis=0),
        jnp.concatenate([stale_v, first_v[:lead]], axis=0),
    ]
    for i in range(3):
        kt3[i] = own_k[i].T
        v3[i, :, :CP] = own_v[i]
    rest = KEYS - FIRST
    kt[:, :rest] = jnp.concatenate([first_k[lead:], second_k], axis=0).T
    vb[: 2 * MINE - lead, :CP] = first_v[lead:]
    vb[2 * MINE - lead : rest, :CP] = second_v

    lane128 = lax.broadcasted_iota(jnp.int32, (1, 128), 1)
    low_half = lane128 < HEAD
    q_copy.wait_recv()
    for who in range(2):
        for h in range(HEADS):
            slab = qcomp[who, :, (h // 2) * 128 : (h // 2) * 128 + 128]
            keep = low_half if h % 2 == 0 else jnp.logical_not(low_half)
            qz[h, who * MINE : (who + 1) * MINE, :] = jnp.where(keep, slab, jnp.zeros_like(slab))

    def attend(scores_of, values_of, first, between):
        scores = scores_of(0)
        for h in range(HEADS):
            following = scores_of(h + 1) if h < HEADS - 1 else None
            peak = jnp.max(scores, axis=1, keepdims=True)
            if not first:
                old = m_ref[h][:, :1]
                peak = jnp.maximum(old, peak)
            weights = jnp.exp2(scores - peak).astype(BF16)
            m_ref[h] = jnp.broadcast_to(peak, (BOTH, 128))
            if first:
                acc_ref[h] = values_of(h, weights)
            else:
                acc_ref[h] = acc_ref[h] * jnp.exp2(old - peak) + values_of(h, weights)
            scores = following
            if h in between:
                between[h]()

    parts = ((0, 0, BAND), (1, BAND, MINE), (2, MINE, BOTH))

    def own_scores(h):
        s = h // 2 * 128
        own = jnp.concatenate([dot(qz[h, a:b], kt3[i, s : s + 128]) for i, a, b in parts], axis=0)
        return jnp.concatenate([own, dot(qz[h], kt[s : s + 128, :rest])], axis=1)

    def own_values(h, weights):
        s = h // 2 * 128
        own = jnp.concatenate(
            [
                dot(weights[a:b, :FIRST], jnp.concatenate([v3[i, :, s : s + 128], v3[i, :, CP:]], axis=1))
                for i, a, b in parts
            ],
            axis=0,
        )
        return own + dot(weights[:, FIRST:], jnp.concatenate([vb[:rest, s : s + 128], vb[:rest, CP:]], axis=1))

    def middle():
        pass_right(2, 1)
        pass_left(2, 0)

    def late():
        to_right(3, 0).wait_recv()
        far_right().start()
        to_left(3, 1).wait_recv()
        far_left().start()

    attend(own_scores, own_values, True, {1: middle, 3: late})

    to_right(3, 1).wait_recv()
    to_left(3, 0).wait_recv()
    k, v = project([(2, 1), (5, 0), (3, 0), (3, 1), (6, 0), (6, 1)])
    kb[: 6 * BAND] = k
    vb[: 6 * BAND, :CP] = v
    far_right().wait_recv()
    far_left().wait_recv()
    k, v = project([(7, 0), (7, 1)])
    kb[6 * BAND :] = k
    vb[6 * BAND :, :CP] = v
    kt[...] = kb[...].T

    def scores_of(h):
        s = h // 2 * 128
        return dot(qz[h], kt[s : s + 128])

    def values_of(h, weights):
        s = h // 2 * 128
        return dot(weights, jnp.concatenate([vb[:, s : s + 128], vb[:, CP:]], axis=1))

    attend(scores_of, values_of, False, {})

    notes = jnp.zeros((MINE, 128), F32)
    for h in range(HEADS):
        notes = jnp.where(lane128 == h, m_ref[h, MINE:], notes)
        notes = jnp.where(lane128 == 8 + h, acc_ref[h, MINE:, 128:], notes)
    for slab in range(3):
        one = acc_ref[2 * slab, MINE:, :128]
        if slab < 2:
            one = jnp.where(low_half, one, acc_ref[2 * slab + 1, MINE:, :128])
        msend[:, slab * 128 : (slab + 1) * 128] = one
    msend[:, CP:] = notes
    merge = remote(msend, mrecv, mg_sems.at[0], mg_sems.at[1], twin)
    merge.start()

    for parity in range(2):
        remote(st_fin, st_own.at[parity], own_send.at[0], own_recv.at[parity], sides[0]).wait_recv()
        factors = [factor_row(ex_ref, parity, r) for r in range(2)]
        columns = rows_of(st_own[parity, 0:1], st_own[parity, 1:2], gain, bias, shift, *factors).T
        mean_c, rstd_c, gain_c, bias_c, shift_c = [columns[:, i : i + 1] for i in range(5)]
        for r in range(2):
            factor_c = columns[:, 5 + r : 6 + r]
            own = lat_ref[parity, r].astype(F32)
            normed_own = ((own - mean_c) * rstd_c * gain_c + bias_c + shift_c).astype(BF16).astype(F32)
            stale_own = code_ref[parity, r].astype(F32) * factor_c
            res_ref[parity, r] = ((normed_own - stale_own) / factor_c).astype(BF16)

    merge.wait_recv()
    keep_own, keep_other, sums = [], [], []
    for h in range(HEADS):
        mine, other = m_ref[h, :MINE], mrecv[:, CP + h : CP + h + 1]
        peak = jnp.maximum(mine, other)
        a, b = jnp.exp2(mine - peak), jnp.exp2(other - peak)
        keep_own.append(a)
        keep_other.append(b)
        sums.append(acc_ref[h, :MINE, 128:] * a + mrecv[:, CP + 8 + h : CP + 9 + h] * b)
    slabs = []
    for slab in range(3):
        e, o = 2 * slab, min(2 * slab + 1, HEADS - 1)

        def pick(values):
            return values[e] if e == o else jnp.where(low_half, values[e], values[o])

        own_sum = pick([acc_ref[h, :MINE, :128] for h in range(HEADS)])
        joined = own_sum * pick(keep_own) + mrecv[:, slab * 128 : (slab + 1) * 128] * pick(keep_other)
        slabs.append((joined / pick(sums)).astype(BF16))
    attended = jnp.concatenate(slabs, axis=1)
    sec[...] = (wide_ref[...].astype(F32) + dot(attended, woutp[...])).astype(BF16)

    def forward(j, source):
        return remote(
            sec.at[pl.ds(j * CELLS, CELLS)], xin.at[source], f_send.at[j], f_recv.at[source],
            worker_device(j, z, core),
        )

    for k in range(1, FRAMES):
        j = (frame + k) % FRAMES

        @pl.when(j < WORKERS)
        def _():
            forward(j, frame).start()

    band = frame // 7
    spot = frame % 7
    here = x_lo * 4 + y

    def back(target):
        return remote(
            yout.at[pl.ds(2 * target, 2)],
            got.at[pl.ds(0, 2), pl.ds(spot * CELLS, CELLS)],
            b_send.at[target],
            b_recv.at[spot],
            device(target // 4, target % 4, z, band, core),
        )

    def back_local(target):
        return pltpu.make_async_copy(
            yout.at[pl.ds(2 * target, 2)], got.at[pl.ds(0, 2), pl.ds(spot * CELLS, CELLS)], local_sem.at[1]
        )

    @pl.when(frame < WORKERS)
    def _():
        to_self = pltpu.make_async_copy(sec.at[pl.ds(frame * CELLS, CELLS)], xin.at[frame], local_sem.at[0])
        to_self.start()
        for k in range(1, FRAMES):
            forward(0, (frame + k) % FRAMES).wait_recv()
        to_self.wait()

        tile = FRAMES * 16
        row_cell = lax.broadcasted_iota(jnp.int32, (tile, tile), 0) % 16
        col_cell = lax.broadcasted_iota(jnp.int32, (tile, tile), 1) % 16
        same = row_cell == col_cell
        for part in range(CELLS // 16):
            section = xin[:, part * 16 : (part + 1) * 16, :].astype(F32)
            shifted = (section + embed_ref[...][:, None, :]).reshape(tile, C)
            mean = jnp.mean(shifted, axis=-1, keepdims=True)
            deviation = shifted - mean
            normed = (
                deviation * lax.rsqrt(jnp.mean(deviation * deviation, axis=-1, keepdims=True) + 1e-05)
            ).astype(BF16)
            proj = dot(normed, wp[...]).astype(BF16)
            mixed = []
            for slab in range(3):
                q = proj[:, slab * 128 : (slab + 1) * 128]
                k = proj[:, CP + slab * 128 : CP + (slab + 1) * 128]
                v = proj[:, 2 * CP + slab * 128 : 2 * CP + (slab + 1) * 128]
                halves = []
                for h in range(2 if slab < 2 else 1):
                    keep = low_half if h == 0 else jnp.logical_not(low_half)
                    scores = lax.dot_general(
                        jnp.where(keep, q, jnp.zeros_like(q)), k, (((1,), (1,)), ((), ())),
                        preferred_element_type=F32,
                    ) * (HEAD**-0.5)
                    scores = jnp.where(same, scores, -1e30)
                    weights = jnp.exp(scores - jnp.max(scores, axis=1, keepdims=True))
                    below = jnp.sum(weights, axis=1, keepdims=True)
                    halves.append(dot(weights.astype(BF16), v) / below)
                mixed.append(halves[0] if slab == 2 else jnp.where(low_half, halves[0], halves[1]))
            mix = jnp.concatenate(mixed, axis=1).astype(BF16)
            result = section.reshape(tile, C) + dot(mix, wtoutp[...])
            yout[:, part * 16 : (part + 1) * 16, :] = result.astype(BF16).reshape(FRAMES, 16, C)
        for k in range(8):
            target = (here + k) % 8
            stays = jnp.logical_and(k == 0, x_hi == band)

            @pl.when(stays)
            def _():
                back_local(target).start()

            @pl.when(jnp.logical_not(stays))
            def _():
                back(target).start()

    for s in range(7):
        source = x_hi * 7 + s

        @pl.when(frame == source)
        def _():
            pltpu.make_async_copy(
                yout.at[pl.ds(0, 2)], got.at[pl.ds(0, 2), pl.ds(s * CELLS, CELLS)], local_sem.at[1]
            ).wait()

        @pl.when(frame != source)
        def _():
            remote(
                yout.at[pl.ds(0, 2)], got.at[pl.ds(0, 2), pl.ds(s * CELLS, CELLS)],
                b_send.at[0], b_recv.at[s], twin,
            ).wait_recv()

    for parity in range(2):
        for r in range(2):
            out_ref[parity, r] = got[parity, r * W : (r + 1) * W, :].astype(F32).T.astype(BF16)

    for parity in range(2):
        lat_copy(parity, x_hi).wait_send()
        code_copy(parity, x_hi).wait_send()
    to_twin.wait_send()
    for copy in z_copies + side_copies + own_copies:
        copy.wait_send()
    q_copy.wait_send()
    merge.wait_send()
    for step in range(1, 4):
        for b in range(2):
            to_right(step, b).wait_send()
            to_left(step, b).wait_send()
    far_right().wait_send()
    far_left().wait_send()
    for k in range(1, FRAMES):
        j = (frame + k) % FRAMES

        @pl.when(j < WORKERS)
        def _():
            forward(j, frame).wait_send()

    @pl.when(frame < WORKERS)
    def _():
        for k in range(8):

            @pl.when(jnp.logical_not(jnp.logical_and(k == 0, x_hi == band)))
            def _():
                back((here + k) % 8).wait_send()


def frame_table():
    half = C // 2
    frequency = np.exp(-math.log(10000.0) * np.arange(half) / half)
    angles = np.arange(FRAMES)[:, None] * frequency
    return np.concatenate([np.cos(angles), np.sin(angles)], axis=-1).astype(np.float32)


VM = pl.BlockSpec(memory_space=pltpu.VMEM)
SM = pl.BlockSpec(memory_space=pltpu.SMEM)


def body(
    latent, timestep, time_weight, norm_gain, norm_bias, spatial_qkv, spatial_out,
    stale_codes, stale_exponents, temporal_qkv, temporal_out,
):
    dma = pltpu.SemaphoreType.DMA
    cells_last = jax.ShapeDtypeStruct((2, 2, C, W), BF16)
    output, residual = pl.pallas_call(
        kernel,
        out_shape=(cells_last, cells_last),
        in_specs=[SM, SM] + [VM] * 10,
        out_specs=(VM, VM),
        scratch_shapes=[
            pltpu.VMEM((2, 2, C, W), BF16),
            pltpu.VMEM((MINE, C), BF16),
            pltpu.VMEM((2, PACK, 128), BF16),
            pltpu.VMEM((ZS, 2, PACK, 128), BF16),
            pltpu.VMEM((8, C), F32),
            pltpu.VMEM((8, C), F32),
            pltpu.VMEM((8, C), F32),
            pltpu.VMEM((ZS, 8, C), F32),
            pltpu.VMEM((2, 8, C), F32),
            pltpu.VMEM((2, 8, C), F32),
            pltpu.VMEM((8, C), F32),
            pltpu.VMEM((2, 8, C), F32),
            pltpu.VMEM((256, 2 * CP), BF16),
            pltpu.VMEM((128, 2 * CP), BF16),
            pltpu.VMEM((128, 2 * CP), BF16),
            pltpu.VMEM((C, CP), BF16),
            pltpu.VMEM((CP, C), BF16),
            pltpu.VMEM((C, 3 * CP), BF16),
            pltpu.VMEM((CP, C), BF16),
            pltpu.VMEM((2, MINE, CP), BF16),
            pltpu.VMEM((HEADS, BOTH, 128), BF16),
            pltpu.VMEM((KEYS, CP), BF16),
            pltpu.VMEM((CP, KEYS), BF16),
            pltpu.VMEM((KEYS, 512), BF16),
            pltpu.VMEM((3, CP, FIRST), BF16),
            pltpu.VMEM((3, FIRST, 512), BF16),
            pltpu.VMEM((HEADS, BOTH, 128), F32),
            pltpu.VMEM((HEADS, BOTH, 256), F32),
            pltpu.VMEM((MINE, 512), F32),
            pltpu.VMEM((MINE, 512), F32),
            pltpu.VMEM((MINE, C), BF16),
            pltpu.VMEM((FRAMES, CELLS, C), BF16),
            pltpu.VMEM((FRAMES, CELLS, C), BF16),
            pltpu.VMEM((2, BAND, C), BF16),
            dma((4,)), dma((2,)), dma((2,)), dma((7,)), dma((7,)), dma((7,)), dma((7,)),
            dma((2,)), dma((ZS,)), dma((ZS,)), dma((2,)), dma((2,)), dma((2,)), dma((2,)),
            dma((2,)), dma((2,)),
            dma((FRAMES,)), dma((FRAMES,)), dma((8,)), dma((7,)), dma((2,)),
        ],
        compiler_params=pltpu.CompilerParams(
            collective_id=0, has_side_effects=True, vmem_limit_bytes=60 * 2**20
        ),
        name="block",
    )(
        timestep, stale_exponents, jnp.transpose(latent, (0, 1, 3, 2)), jnp.transpose(stale_codes, (0, 1, 3, 2)),
        time_weight, norm_gain, norm_bias, spatial_qkv, spatial_out, jnp.asarray(frame_table()),
        temporal_qkv, temporal_out,
    )
    return jnp.transpose(output, (0, 1, 3, 2)), jnp.transpose(residual, (0, 1, 3, 2))


def solution(mesh):
    placed = (
        P("frame", "patch", None, None),
        P(),
        P(),
        P(),
        P(),
        P(),
        P(),
        P("frame", "patch", None, None),
        P("frame", "patch", None),
        P(),
        P(),
    )
    return jax.shard_map(
        body,
        mesh=mesh,
        in_specs=placed,
        out_specs=(P("frame", "patch", None, None), P("frame", "patch", None, None)),
        check_vma=False,
    )
```

time: 102 us -> 83.4 us (0.82)
  Pallas kernels: 92.3 us -> 78.9 us
  local copies, waits for them, and re-layouts: 7.5 us -> 2.49 us
    pallas_call x2 -> x1, Pallas kernels: 92.3 us -> 78.9 us  [body(): pl.pallas_call(kernel, out_shape=(cells_last, cells_last), in_specs=[SM,...]
    unnamed x18 -> x4, local copies, waits for them, and re-layouts: 5.69 us -> 2.49 us
    reshape x2 -> x0, local copies, waits for them, and re-layouts: 1.81 us -> none  [the longest x1 1.25 us: body(): norm_gain.reshape(1, C)]
where the time goes in v2:
time: 83.4 us; the launch traced here: 82.7 us
  Pallas kernels  78.9 us (95%)
  local copies, waits for them, and re-layouts  2.49 us (3%)
  between operations  1.3 us (2%)
    pallas_call x1, Pallas kernels, body(): pl.pallas_call(kernel, out_shape=(cells_last, cells_last), in_specs=[SM,...  78.9 us
    unnamed x4, local copies, waits for them, and re-layouts  2.49 us

profile of v2, /device:TPU:30, one launch (start us, length us, event | category | flops | bytes accessed | tf_op | source)
XLA Modules:
  0.0 82.7 jit_solution(16239447854866001130)
XLA Ops:
  1.3 78.9 %block.1 = (bf16[2,2,320,112]{3,2,1,0:T(8,128)(2,1)}, bf16[2,2,320,112]{3,2,1,0:T(8,128)(2,1)}) custom-call(s32[1]{0:T(128)S(6)} %copy.16.ts_ref, s32[2,2,5]{2,1,0:T(2,128)} %ex_ref.1, bf16[2,2,320,112]{3,2,1,0:T(8,128)(2,1)} %bitcast.4, bf16[2,2,320,112]{3,2,1,0:T(8,128)(2,1)} %bitcast.5, bf16[320,320]{1,0:T(8,128)(2,1)} %tw_ref.1, f32[320]{0:T(512)} %gain_ref.1, ...), custom_call_target="tpu_custom_call" | custom-call | tf_op jit(solution)/shard_map/block/pallas_call | solution.py:586
  80.2 0.0 copy-start
  80.2 1.8 %copy.17 = bf16[2,2,112,320]{2,3,1,0:T(8,128)(2,1)} copy(bf16[2,2,112,320]{2,3,1,0:T(8,128)(2,1)} %bitcast.7) | data formatting | bytes 573440
  82.0 0.0 copy-done
  82.0 0.7 copy.18
Async XLA Ops:
  80.2 1.8 %copy-start = (bf16[2,2,320,112]{3,2,1,0:T(8,128)(2,1)S(1)}, bf16[2,2,320,112]{3,2,1,0:T(8,128)(2,1)}, u32[]{:S(2)}) copy-start(bf16[2,2,320,112]{3,2,1,0:T(8,128)(2,1)} %get-tuple-element.5) | copy-start | bytes 860164

commit v3 on v2

v3 whole, which is shorter than its diff:
```python
import functools
import math

import jax
import jax.numpy as jnp
import numpy as np
from jax import lax
from jax.experimental import pallas as pl
from jax.experimental.pallas import tpu as pltpu
from jax.sharding import PartitionSpec as P

HEAD = 64
HEADS = 5
C = 320
CP = 384
GROUP_WIDTH = 10
FRAMES = 16
ROWS = 64
W = 112
BAND = 224
MINE = 2 * BAND
BOTH = 2 * MINE
ZS = 8
PACK = 560
PIECES = ((0, 288), (288, 272))
CELLS = 16
WORKERS = 14
FIRST = 512
LONG = 1280
LAST = 1024
MESH = pl.DeviceIdType.MESH
F32 = jnp.float32
BF16 = jnp.bfloat16
LOG2E = 1.4426950408889634


def dot(a, b):
    return jnp.dot(a, b, preferred_element_type=F32)


def place():
    f, p = lax.axis_index("frame"), lax.axis_index("patch")
    return f // 4, f % 4, p // 4, (p // 2) % 2, p % 2


def device(x_lo, y, z, x_hi, core):
    return (x_lo * 4 + y, z * 4 + x_hi * 2 + core)


def remote(src, dst, send, recv, target):
    return pltpu.make_async_remote_copy(
        src_ref=src, dst_ref=dst, send_sem=send, recv_sem=recv, device_id=target, device_id_type=MESH
    )


def factor_row(ex_ref, frame, row):
    lane = lax.broadcasted_iota(jnp.int32, (1, C), 1) // HEAD
    power = jnp.zeros((1, C), jnp.int32)
    for block in range(C // HEAD):
        power = jnp.where(lane == block, ex_ref[frame, row, block], power)
    out = jnp.full((1, C), 1.0, F32)
    for e in (-1, 1, 2):
        out = jnp.where(power == e, 2.0**e, out)
    return out


def rows_of(*parts):
    row = lax.broadcasted_iota(jnp.int32, (8, C), 0)
    out = jnp.zeros((8, C), F32)
    for i, part in enumerate(parts):
        out = jnp.where(row == i, part, out)
    return out


def worker_device(j, z, core):
    owner = j // 2
    return device(1 - owner // 4, owner % 4, z, j % 2, core)


def kernel(
    ts_ref, ex_ref, lat_ref, code_ref, gain_ref, bias_ref, embed_ref,
    tw_hbm, wqkv_hbm, wout_hbm, wt_hbm, wtout_hbm,
    out_ref, res_ref,
    tw_ref, wqkv_ref, wout_ref, wt_ref, wtout_ref,
    lat_in, wide_ref, stage, ring, st_mine, st_side, st_x, st_all, st_fin, st_own,
    w01, wlo, whi, wq, woutp, wp, wtoutp, qcomp, qz, kb, kt, vb, kt3, v3, m_ref, acc_ref, msend, mrecv, nsend, nrecv,
    sec, xin, yout, same_group,
    w_sems, x_send, lat_recv, code_send, code_recv, rs_right, rs_left, rr_right, rr_left,
    sx_send, sx_recv, all_send, all_recv, own_send, own_recv, q_sems, mg_send, mg_recv,
    f_send, f_recv, b_send, b_recv, local_sem,
):
    x_lo, y, z, x_hi, core = place()
    frame = 2 * ((1 - x_lo) * 4 + y) + x_hi
    twin = device(x_lo, y, z, x_hi, 1 - core)
    right = device(x_lo, y, (z + 1) % ZS, x_hi, core)
    left = device(x_lo, y, (z + ZS - 1) % ZS, x_hi, core)
    sides = [device(1 - x_lo, y, z, parity, core) for parity in range(2)]
    zcores = [
        device(x_lo, y, (z + d // 2) % ZS, x_hi, (core + d) % 2) for d in range(1, 2 * ZS)
    ]

    weight_copies = [
        pltpu.make_async_copy(src, dst, w_sems.at[i])
        for i, (src, dst) in enumerate(
            ((wqkv_hbm, wqkv_ref), (tw_hbm, tw_ref), (wout_hbm, wout_ref), (wt_hbm, wt_ref), (wtout_hbm, wtout_ref))
        )
    ]
    barrier = pltpu.get_barrier_semaphore()
    plane = [worker_device((frame + k) % FRAMES, z, core) for k in range(1, FRAMES)]
    for peer in zcores + plane:
        pl.semaphore_signal(barrier, inc=1, device_id=peer, device_id_type=MESH)
    for copy in weight_copies:
        copy.start()

    for parity in range(2):
        rows = [
            code_ref[parity, r].astype(F32).T * factor_row(ex_ref, parity, r) for r in range(2)
        ]
        for r in range(2):
            for slab in range(2):
                stage[parity, slab * BAND + r * W : slab * BAND + (r + 1) * W, :] = rows[r][
                    :, slab * 128 : (slab + 1) * 128
                ].astype(BF16)
        stage[parity, 2 * BAND :, :] = jnp.concatenate(
            [rows[0][:, 256:320], rows[1][:, 256:320]], axis=1
        ).astype(BF16)

    pl.semaphore_wait(barrier, 2 * ZS - 1 + FRAMES - 1)

    def side_copy(parity, band):
        return remote(st_side.at[parity], st_x.at[band], sx_send.at[parity], sx_recv.at[band], sides[parity])

    def lat_copy(parity, band):
        return remote(lat_ref.at[parity], lat_in.at[band], x_send.at[parity], lat_recv.at[band], sides[parity])

    def code_copy(parity, band, piece):
        rows = pl.ds(*PIECES[piece])
        return remote(
            stage.at[parity, rows], ring.at[0, band, rows],
            code_send.at[parity, piece], code_recv.at[band, piece], sides[parity],
        )

    for piece in range(2):
        for parity in range(2):
            code_copy(parity, x_hi, piece).start()
    local = []
    for parity in range(2):
        own = jnp.concatenate([lat_ref[parity, r].astype(F32).T for r in range(2)], axis=0)
        mean = jnp.sum(own, axis=0, keepdims=True) / BAND
        deviation = own - mean
        local += [mean, jnp.sum(deviation * deviation, axis=0, keepdims=True)]
    st_mine[...] = rows_of(*local)
    all_copies = [
        remote(st_mine, st_all.at[d], all_send.at[d], all_recv.at[d], zcores[d - 1]) for d in range(1, 2 * ZS)
    ]
    for copy in all_copies:
        copy.start()

    for copy in weight_copies:
        copy.wait()
    pad = jnp.zeros((C, CP - C), BF16)
    wq[...] = jnp.concatenate([wqkv_ref[:, :C], pad], axis=1)
    wkv = jnp.concatenate([wqkv_ref[:, C : 2 * C], pad, wqkv_ref[:, 2 * C :], pad], axis=1)
    w01[...] = wkv[:256]
    wlo[:64] = wkv[256:]
    wlo[64:] = jnp.zeros((64, 2 * CP), BF16)
    whi[:64] = jnp.zeros((64, 2 * CP), BF16)
    whi[64:] = wkv[256:]
    vb[:, CP:] = jnp.ones((LONG, 128), BF16)
    for i in range(3):
        v3[i, :, CP:] = jnp.ones((FIRST, 128), BF16)

    same_group[...] = (
        lax.broadcasted_iota(jnp.int32, (C, C), 0) // GROUP_WIDTH
        == lax.broadcasted_iota(jnp.int32, (C, C), 1) // GROUP_WIDTH
    ).astype(F32).astype(BF16)

    for copy in all_copies:
        copy.wait_recv()
    for parity in range(2):
        i = 2 * parity
        means = [st_mine[i : i + 1]] + [st_all[d, i : i + 1] for d in range(1, 2 * ZS)]
        total = sum(means[1:], means[0]) / (2 * ZS)
        squares = st_mine[i + 1 : i + 2]
        for d in range(1, 2 * ZS):
            squares = squares + st_all[d, i + 1 : i + 2]
        for one in means:
            squares = squares + (one - total) * (one - total) * BAND
        st_side[parity] = rows_of(total, squares)
        side_copy(parity, x_hi).start()
    for parity in range(2):
        lat_copy(parity, x_hi).start()

    def to_right(step, band):
        return remote(
            ring.at[step - 1, band], ring.at[step, band],
            rs_right.at[(step - 1) * 2 + band], rr_right.at[(step - 1) * 2 + band], right,
        )

    def to_left(step, band):
        return remote(
            ring.at[0 if step == 1 else step + 2, band], ring.at[step + 3, band],
            rs_left.at[(step - 1) * 2 + band], rr_left.at[(step - 1) * 2 + band], left,
        )

    def far_right():
        return remote(ring.at[3, 0], ring.at[7, 0], rs_right.at[6], rr_right.at[6], right)

    def far_left():
        return remote(ring.at[6, 1], ring.at[7, 1], rs_left.at[6], rr_left.at[6], left)

    def first_hop(band, piece, to, send, recv, slot):
        rows = pl.ds(*PIECES[piece])
        return remote(
            ring.at[0, band, rows], ring.at[slot, band, rows], send.at[band], recv.at[band], to
        )

    for piece in range(2):
        code_copy(0, 0, piece).wait_recv()
        first_hop(0, piece, right, rs_right, rr_right, 1).start()
        code_copy(0, 1, piece).wait_recv()
        first_hop(1, piece, left, rs_left, rr_left, 4).start()
    for piece in range(2):
        first_hop(1, piece, right, rs_right, rr_right, 1).start()
        first_hop(0, piece, left, rs_left, rr_left, 4).start()

    def project(blocks):
        x01 = jnp.concatenate(
            [jnp.concatenate([ring[s, b, :BAND], ring[s, b, BAND : 2 * BAND]], axis=1) for s, b in blocks], axis=0
        )
        tail = jnp.concatenate([ring[s, b, 2 * BAND :] for s, b in blocks], axis=0)
        low, high = dot(tail, wlo[...]), dot(tail, whi[...])
        rest = []
        for i in range(len(blocks)):
            rest += [low[i * W : (i + 1) * W], high[i * W : (i + 1) * W]]
        both = (dot(x01, w01[...]) + jnp.concatenate(rest, axis=0)).astype(BF16)
        return both[:, :CP], both[:, CP:]

    stale_k, stale_v = project([(0, 0), (0, 1)])

    woutp[:C] = wout_ref[...]
    woutp[C:] = jnp.zeros((CP - C, C), BF16)
    wp[...] = jnp.concatenate([wt_ref[:, :C], pad, wt_ref[:, C : 2 * C], pad, wt_ref[:, 2 * C :], pad], axis=1)
    wtoutp[:C] = wtout_ref[...]
    wtoutp[C:] = jnp.zeros((CP - C, C), BF16)

    lane = lax.broadcasted_iota(jnp.int32, (1, C), 1)
    half = C // 2
    index = jnp.where(lane < half, lane, lane - half).astype(F32)
    angle = ts_ref[0].astype(F32) * jnp.exp(-math.log(10000.0) * index / half)
    embed = jnp.where(lane < half, jnp.cos(angle), jnp.sin(angle)).astype(BF16)
    shift = dot(jnp.broadcast_to(embed, (16, C)), tw_ref[...])[0:1]
    gain = gain_ref[...].reshape(1, C)
    bias = bias_ref[...].reshape(1, C)

    for band in range(2):
        side_copy(0, band).wait_recv()
    total = (st_x[0, 0:1] + st_x[1, 0:1]) * 0.5
    delta = st_x[0, 0:1] - st_x[1, 0:1]
    cells = ROWS * W
    squares = st_x[0, 1:2] + st_x[1, 1:2] + delta * delta * (cells / 4)

    def group_sum(row):
        high = row.astype(BF16)
        left_over = row - high.astype(F32)
        middle = left_over.astype(BF16)
        low = (left_over - middle.astype(F32)).astype(BF16)
        sums = dot(
            jnp.concatenate([jnp.broadcast_to(part, (16, C)) for part in (high, middle, low)], axis=0),
            same_group[...],
        )
        return sums[0:1] + sums[16:17] + sums[32:33]

    group_mean = group_sum(total) / GROUP_WIDTH
    off = total - group_mean
    group_var = group_sum(squares + off * off * cells) / (cells * GROUP_WIDTH)
    rstd = lax.rsqrt(group_var + 1e-05)
    st_fin[...] = rows_of(group_mean, rstd)
    own_copies = [
        remote(st_fin, st_own.at[x_hi], own_send.at[i], own_recv.at[x_hi], sides[i]) for i in range(2)
    ]
    for copy in own_copies:
        copy.start()

    for band in range(2):
        lat_copy(0, band).wait_recv()
        for r in range(2):
            wide_ref[band * BAND + r * W : band * BAND + (r + 1) * W] = (
                lat_in[band, r].astype(F32).T.astype(BF16)
            )
    wide = wide_ref[...].astype(F32)
    normed = ((wide - group_mean) * rstd * gain + bias + shift).astype(BF16)
    qcomp[0] = (dot(normed, wq[...]) * (HEAD**-0.5 * LOG2E)).astype(BF16)
    q_copy = remote(qcomp.at[0], qcomp.at[1], q_sems.at[0], q_sems.at[1], twin)
    q_copy.start()
    fresh = (dot(normed[:, :256], w01[...]) + dot(normed[:, 256:], wlo[:64])).astype(BF16)
    fresh_k, fresh_v = fresh[:, :CP], fresh[:, CP:]

    def pass_right(step, band):
        to_right(step, band).wait_recv()
        to_right(step + 1, band).start()

    def pass_left(step, band):
        to_left(step, band).wait_recv()
        to_left(step + 1, band).start()

    pass_right(1, 0)
    pass_left(1, 1)
    near_k, near_v = project([(1, 0), (4, 1)])
    lead = FIRST - MINE
    rest = LONG - FIRST
    own_k = [
        jnp.concatenate([fresh_k[:BAND], stale_k[BAND:], near_k[:lead]], axis=0),
        jnp.concatenate([stale_k[:BAND], fresh_k[BAND:], near_k[:lead]], axis=0),
        jnp.concatenate([stale_k, near_k[:lead]], axis=0),
    ]
    own_v = [
        jnp.concatenate([fresh_v[:BAND], stale_v[BAND:], near_v[:lead]], axis=0),
        jnp.concatenate([stale_v[:BAND], fresh_v[BAND:], near_v[:lead]], axis=0),
        jnp.concatenate([stale_v, near_v[:lead]], axis=0),
    ]
    for i in range(3):
        kt3[i] = own_k[i].T
        v3[i, :, :CP] = own_v[i]

    lane128 = lax.broadcasted_iota(jnp.int32, (1, 128), 1)
    low_half = lane128 < HEAD
    q_copy.wait_recv()
    for who in range(2):
        for h in range(HEADS):
            slab = qcomp[who, :, (h // 2) * 128 : (h // 2) * 128 + 128]
            keep = low_half if h % 2 == 0 else jnp.logical_not(low_half)
            slab = jnp.where(keep, slab, jnp.zeros_like(slab))
            for b in range(2):
                qz[h, b * MINE + who * BAND : b * MINE + (who + 1) * BAND, :] = slab[b * BAND : (b + 1) * BAND]

    pass_right(1, 1)
    pass_left(1, 0)
    next_k, next_v = project([(1, 1), (4, 0)])
    first_k = jnp.concatenate([near_k, next_k], axis=0)
    first_v = jnp.concatenate([near_v, next_v], axis=0)
    kt[:, :rest] = first_k[lead : lead + rest].T
    vb[:rest, :CP] = first_v[lead : lead + rest]

    def attend(items, scores_of, values_of, first, between):
        scores = scores_of(*items[0])
        for n, (h, a, b) in enumerate(items):
            following = scores_of(*items[n + 1]) if n + 1 < len(items) else None
            peak = jnp.max(scores, axis=1, keepdims=True)
            if not first:
                old = m_ref[h, a:b][:, :1]
                peak = jnp.maximum(old, peak)
            weights = jnp.exp2(scores - peak).astype(BF16)
            m_ref[h, a:b] = jnp.broadcast_to(peak, (b - a, 128))
            if first:
                acc_ref[h, a:b] = values_of(h, weights)
            else:
                acc_ref[h, a:b] = acc_ref[h, a:b] * jnp.exp2(old - peak) + values_of(h, weights)
            scores = following
            if n in between:
                between[n]()

    def all_heads(a, b):
        return [(h, a, b) for h in range(HEADS)]

    parts = ((0, 0, BAND), (2, BAND, MINE), (1, MINE, MINE + BAND), (2, MINE + BAND, BOTH))

    def own_scores(h, start, stop):
        s = h // 2 * 128
        own = jnp.concatenate([dot(qz[h, a:b], kt3[i, s : s + 128]) for i, a, b in parts], axis=0)
        return jnp.concatenate([own, dot(qz[h, start:stop], kt[s : s + 128, :rest])], axis=1)

    def own_values(h, weights):
        s = h // 2 * 128
        own = jnp.concatenate(
            [
                dot(weights[a:b, :FIRST], jnp.concatenate([v3[i, :, s : s + 128], v3[i, :, CP:]], axis=1))
                for i, a, b in parts
            ],
            axis=0,
        )
        return own + dot(weights[:, FIRST:], jnp.concatenate([vb[:rest, s : s + 128], vb[:rest, CP:]], axis=1))

    def second_first():
        pass_right(2, 0)
        pass_left(2, 1)

    def second_last():
        pass_right(2, 1)
        pass_left(2, 0)

    attend(all_heads(0, BOTH), own_scores, own_values, True, {0: second_first, 2: second_last})

    def chunk(keys, items, between):
        def scores_of(h, a, b):
            s = h // 2 * 128
            return dot(qz[h, a:b], kt[s : s + 128, :keys])

        def values_of(h, weights):
            s = h // 2 * 128
            return dot(weights, jnp.concatenate([vb[:keys, s : s + 128], vb[:keys, CP:]], axis=1))

        attend(items, scores_of, values_of, False, between)

    left_k, left_v = first_k[lead + rest :], first_v[lead + rest :]
    count = left_k.shape[0]
    kb[:count] = left_k
    vb[:count, :CP] = left_v
    k, v = project([(2, 0), (5, 1), (2, 1), (5, 0)])
    kb[count : count + BOTH] = k
    vb[count : count + BOTH, :CP] = v
    count += BOTH
    to_right(3, 0).wait_recv()
    far_right().start()
    to_left(3, 1).wait_recv()
    far_left().start()
    k, v = project([(3, 0), (6, 1)])
    kb[count:] = k[: LONG - count]
    vb[count:, :CP] = v[: LONG - count]
    left_k, left_v = k[LONG - count :], v[LONG - count :]
    kt[...] = kb[...].T
    chunk(LONG, all_heads(0, BOTH), {})

    count = left_k.shape[0]
    kb[:count] = left_k
    vb[:count, :CP] = left_v
    to_right(3, 1).wait_recv()
    to_left(3, 0).wait_recv()
    k, v = project([(3, 1), (6, 0)])
    kb[count : count + MINE] = k
    vb[count : count + MINE, :CP] = v
    count += MINE
    far_right().wait_recv()
    far_left().wait_recv()
    k, v = project([(7, 0), (7, 1)])
    kb[count:LAST] = k
    vb[count:LAST, :CP] = v
    kt[:, :LAST] = kb[:LAST].T

    def merge(b):
        return [
            remote(msend.at[b], mrecv.at[b], mg_send.at[b, 0], mg_recv.at[b, 0], twin),
            remote(nsend.at[b], nrecv.at[b], mg_send.at[b, 1], mg_recv.at[b, 1], twin),
        ]

    def give(b):
        rows = slice(b * MINE + BAND, (b + 1) * MINE)
        notes = jnp.zeros((BAND, 128), F32)
        for h in range(HEADS):
            notes = jnp.where(lane128 == h, m_ref[h, rows], notes)
            notes = jnp.where(lane128 == 8 + h, acc_ref[h, rows, 128:], notes)
        for slab in range(3):
            one = acc_ref[2 * slab, rows, :128]
            if slab < 2:
                one = jnp.where(low_half, one, acc_ref[2 * slab + 1, rows, :128])
            msend[b, :, slab * 128 : (slab + 1) * 128] = one.astype(BF16)
        nsend[b] = notes
        for copy in merge(b):
            copy.start()

    def forward(b, j, source):
        return remote(
            sec.at[b, pl.ds(j * CELLS, CELLS)], xin.at[b, source], f_send.at[b, j], f_recv.at[b, source],
            worker_device(j, z, core),
        )

    def to_self(b):
        return pltpu.make_async_copy(
            sec.at[b, pl.ds(frame * CELLS, CELLS)], xin.at[b, frame], local_sem.at[b]
        )

    def take(b):
        rows = slice(b * MINE, b * MINE + BAND)
        for copy in merge(b):
            copy.wait_recv()
        keep_own, keep_other, sums = [], [], []
        for h in range(HEADS):
            mine, other = m_ref[h, rows], nrecv[b, :, h : h + 1]
            peak = jnp.maximum(mine, other)
            own_part, other_part = jnp.exp2(mine - peak), jnp.exp2(other - peak)
            keep_own.append(own_part)
            keep_other.append(other_part)
            sums.append(
                acc_ref[h, rows, 128:] * own_part + nrecv[b, :, 8 + h : 9 + h] * other_part
            )
        slabs = []
        for slab in range(3):
            e, o = 2 * slab, min(2 * slab + 1, HEADS - 1)

            def pick(values):
                return values[e] if e == o else jnp.where(low_half, values[e], values[o])

            own_sum = pick([acc_ref[h, rows, :128] for h in range(HEADS)])
            joined = own_sum * pick(keep_own) + mrecv[b, :, slab * 128 : (slab + 1) * 128].astype(F32) * pick(keep_other)
            slabs.append((joined / pick(sums)).astype(BF16))
        attended = jnp.concatenate(slabs, axis=1)
        sec[b] = (wide_ref[b * BAND : (b + 1) * BAND].astype(F32) + dot(attended, woutp[...])).astype(BF16)
        for k in range(1, FRAMES):
            j = (frame + k) % FRAMES

            @pl.when(j < WORKERS)
            def _():
                forward(b, j, frame).start()

        @pl.when(frame < WORKERS)
        def _():
            to_self(b).start()

    chunk(LAST, all_heads(0, MINE), {})
    give(0)
    chunk(LAST, all_heads(MINE, BOTH), {2: lambda: take(0)})
    give(1)

    for parity in range(2):
        remote(st_fin, st_own.at[parity], own_send.at[0], own_recv.at[parity], sides[0]).wait_recv()
        factors = [factor_row(ex_ref, parity, r) for r in range(2)]
        columns = rows_of(st_own[parity, 0:1], st_own[parity, 1:2], gain, bias, shift, *factors).T
        mean_c, rstd_c, gain_c, bias_c, shift_c = [columns[:, i : i + 1] for i in range(5)]
        for r in range(2):
            factor_c = columns[:, 5 + r : 6 + r]
            own = lat_ref[parity, r].astype(F32)
            normed_own = ((own - mean_c) * rstd_c * gain_c + bias_c + shift_c).astype(BF16).astype(F32)
            stale_own = code_ref[parity, r].astype(F32) * factor_c
            res_ref[parity, r] = ((normed_own - stale_own) / factor_c).astype(BF16)

    take(1)

    here = x_lo * 4 + y

    def back(b, target):
        return remote(
            yout.at[b, pl.ds(2 * target, 2)],
            out_ref.at[pl.ds(0, 2), pl.ds(frame * CELLS, CELLS)],
            b_send.at[b, target],
            b_recv.at[frame],
            device(target // 4, target % 4, z, b, core),
        )

    @pl.when(frame < WORKERS)
    def _():
        tile = FRAMES * CELLS
        row_cell = lax.broadcasted_iota(jnp.int32, (tile, tile), 0) % CELLS
        col_cell = lax.broadcasted_iota(jnp.int32, (tile, tile), 1) % CELLS
        same = row_cell == col_cell
        for b in range(2):
            for k in range(1, FRAMES):
                forward(b, 0, (frame + k) % FRAMES).wait_recv()
            to_self(b).wait()
            section = xin[b].astype(F32)
            shifted = (section + embed_ref[...][:, None, :]).reshape(tile, C)
            mean = jnp.mean(shifted, axis=-1, keepdims=True)
            deviation = shifted - mean
            normed_t = (
                deviation * lax.rsqrt(jnp.mean(deviation * deviation, axis=-1, keepdims=True) + 1e-05)
            ).astype(BF16)
            proj = dot(normed_t, wp[...]).astype(BF16)
            mixed = []
            for slab in range(3):
                q = proj[:, slab * 128 : (slab + 1) * 128]
                k = proj[:, CP + slab * 128 : CP + (slab + 1) * 128]
                v = proj[:, 2 * CP + slab * 128 : 2 * CP + (slab + 1) * 128]
                halves = []
                for h in range(2 if slab < 2 else 1):
                    keep = low_half if h == 0 else jnp.logical_not(low_half)
                    scores = lax.dot_general(
                        jnp.where(keep, q, jnp.zeros_like(q)), k, (((1,), (1,)), ((), ())),
                        preferred_element_type=F32,
                    ) * (HEAD**-0.5)
                    scores = jnp.where(same, scores, -1e30)
                    weights = jnp.exp(scores - jnp.max(scores, axis=1, keepdims=True))
                    below = jnp.sum(weights, axis=1, keepdims=True)
                    halves.append(dot(weights.astype(BF16), v) / below)
                mixed.append(halves[0] if slab == 2 else jnp.where(low_half, halves[0], halves[1]))
            mix = jnp.concatenate(mixed, axis=1).astype(BF16)
            result = section.reshape(tile, C) + dot(mix, wtoutp[...])
            yout[b] = result.astype(BF16).reshape(FRAMES, CELLS, C)
            for k in range(8):
                stays = jnp.logical_and(k == 0, x_hi == b)

                @pl.when(stays)
                def _():
                    pltpu.make_async_copy(
                        yout.at[b, pl.ds(2 * here, 2)],
                        out_ref.at[pl.ds(0, 2), pl.ds(frame * CELLS, CELLS)],
                        local_sem.at[2],
                    ).start()

                @pl.when(jnp.logical_not(stays))
                def _():
                    back(b, (here + k) % 8).start()

    for s in range(WORKERS):

        @pl.when(frame == s)
        def _():
            pltpu.make_async_copy(
                yout.at[0, pl.ds(0, 2)], out_ref.at[pl.ds(0, 2), pl.ds(s * CELLS, CELLS)], local_sem.at[2]
            ).wait()

        @pl.when(frame != s)
        def _():
            remote(
                yout.at[0, pl.ds(0, 2)], out_ref.at[pl.ds(0, 2), pl.ds(s * CELLS, CELLS)],
                b_send.at[0, 0], b_recv.at[s], twin,
            ).wait_recv()

    for parity in range(2):
        for send in (side_copy, lat_copy):
            send(parity, x_hi).wait_send()
        for piece in range(2):
            code_copy(parity, x_hi, piece).wait_send()
    for copy in all_copies + own_copies:
        copy.wait_send()
    q_copy.wait_send()
    for step in range(1, 4):
        for b in range(2):
            to_right(step, b).wait_send()
            to_left(step, b).wait_send()
    far_right().wait_send()
    far_left().wait_send()
    for b in range(2):
        for copy in merge(b):
            copy.wait_send()
        for k in range(1, FRAMES):
            j = (frame + k) % FRAMES

            @pl.when(j < WORKERS)
            def _():
                forward(b, j, frame).wait_send()

    @pl.when(frame < WORKERS)
    def _():
        for b in range(2):
            for k in range(8):

                @pl.when(jnp.logical_not(jnp.logical_and(k == 0, x_hi == b)))
                def _():
                    back(b, (here + k) % 8).wait_send()


def frame_table():
    half = C // 2
    frequency = np.exp(-math.log(10000.0) * np.arange(half) / half)
    angles = np.arange(FRAMES)[:, None] * frequency
    return np.concatenate([np.cos(angles), np.sin(angles)], axis=-1).astype(np.float32)


VM = pl.BlockSpec(memory_space=pltpu.VMEM)
SM = pl.BlockSpec(memory_space=pltpu.SMEM)
HBM = pl.BlockSpec(memory_space=pl.ANY)


def body(
    latent, timestep, time_weight, norm_gain, norm_bias, spatial_qkv, spatial_out,
    stale_codes, stale_exponents, temporal_qkv, temporal_out,
):
    dma = pltpu.SemaphoreType.DMA
    output, residual = pl.pallas_call(
        kernel,
        out_shape=(pltpu.VMEM((2, BAND, C), BF16), pltpu.VMEM((2, 2, C, W), BF16)),
        in_specs=[SM, SM] + [VM] * 5 + [HBM] * 5,
        out_specs=(VM, VM),
        scratch_shapes=[
            pltpu.VMEM((C, C), BF16),
            pltpu.VMEM((C, 3 * C), BF16),
            pltpu.VMEM((C, C), BF16),
            pltpu.VMEM((C, 3 * C), BF16),
            pltpu.VMEM((C, C), BF16),
            pltpu.VMEM((2, 2, C, W), BF16),
            pltpu.VMEM((MINE, C), BF16),
            pltpu.VMEM((2, PACK, 128), BF16),
            pltpu.VMEM((ZS, 2, PACK, 128), BF16),
            pltpu.VMEM((8, C), F32),
            pltpu.VMEM((2, 8, C), F32),
            pltpu.VMEM((2, 8, C), F32),
            pltpu.VMEM((2 * ZS, 8, C), F32),
            pltpu.VMEM((8, C), F32),
            pltpu.VMEM((2, 8, C), F32),
            pltpu.VMEM((256, 2 * CP), BF16),
            pltpu.VMEM((128, 2 * CP), BF16),
            pltpu.VMEM((128, 2 * CP), BF16),
            pltpu.VMEM((C, CP), BF16),
            pltpu.VMEM((CP, C), BF16),
            pltpu.VMEM((C, 3 * CP), BF16),
            pltpu.VMEM((CP, C), BF16),
            pltpu.VMEM((2, MINE, CP), BF16),
            pltpu.VMEM((HEADS, BOTH, 128), BF16),
            pltpu.VMEM((LONG, CP), BF16),
            pltpu.VMEM((CP, LONG), BF16),
            pltpu.VMEM((LONG, 512), BF16),
            pltpu.VMEM((3, CP, FIRST), BF16),
            pltpu.VMEM((3, FIRST, 512), BF16),
            pltpu.VMEM((HEADS, BOTH, 128), F32),
            pltpu.VMEM((HEADS, BOTH, 256), F32),
            pltpu.VMEM((2, BAND, CP), BF16),
            pltpu.VMEM((2, BAND, CP), BF16),
            pltpu.VMEM((2, BAND, 128), F32),
            pltpu.VMEM((2, BAND, 128), F32),
            pltpu.VMEM((2, BAND, C), BF16),
            pltpu.VMEM((2, FRAMES, CELLS, C), BF16),
            pltpu.VMEM((2, FRAMES, CELLS, C), BF16),
            pltpu.VMEM((C, C), BF16),
            dma((5,)), dma((2,)), dma((2,)), dma((2, 2)), dma((2, 2)), dma((7,)), dma((7,)), dma((7,)), dma((7,)),
            dma((2,)), dma((2,)), dma((2 * ZS,)), dma((2 * ZS,)), dma((2,)), dma((2,)), dma((2,)),
            dma((2, 2)), dma((2, 2)),
            dma((2, FRAMES)), dma((2, FRAMES)), dma((2, 8)), dma((WORKERS,)), dma((3,)),
        ],
        compiler_params=pltpu.CompilerParams(
            collective_id=0, has_side_effects=True, vmem_limit_bytes=60 * 2**20
        ),
        name="block",
    )(
        timestep, stale_exponents, jnp.transpose(latent, (0, 1, 3, 2)), jnp.transpose(stale_codes, (0, 1, 3, 2)),
        norm_gain, norm_bias, jnp.asarray(frame_table()),
        time_weight, spatial_qkv, spatial_out, temporal_qkv, temporal_out,
    )
    return output.reshape(2, 2, W, C), jnp.transpose(residual, (0, 1, 3, 2))


def solution(mesh):
    placed = (
        P("frame", "patch", None, None),
        P(),
        P(),
        P(),
        P(),
        P(),
        P(),
        P("frame", "patch", None, None),
        P("frame", "patch", None),
        P(),
        P(),
    )
    return jax.shard_map(
        body,
        mesh=mesh,
        in_specs=placed,
        out_specs=(P("frame", "patch", None, None), P("frame", "patch", None, None)),
        check_vma=False,
    )
```

time: 83.4 us -> 73.4 us (0.88)
  Pallas kernels: 78.9 us -> 70.3 us
  local copies, waits for them, and re-layouts: 2.49 us -> 1.63 us
    pallas_call x1, Pallas kernels: 78.9 us -> 70.3 us  [body(): pl.pallas_call(kernel, out_shape=(pltpu.VMEM((2, BAND, C), BF16), pltpu.V...]
    unnamed x4 -> x2, local copies, waits for them, and re-layouts: 2.49 us -> 1.63 us
where the time goes in v3:
time: 73.4 us; the launch traced here: 73.3 us
  Pallas kernels  70.3 us (96%)
  local copies, waits for them, and re-layouts  1.63 us (2%)
  between operations  1.29 us (2%)
    pallas_call x1, Pallas kernels, body(): pl.pallas_call(kernel, out_shape=(pltpu.VMEM((2, BAND, C), BF16), pltpu.V...  70.3 us
    unnamed x2, local copies, waits for them, and re-layouts  1.63 us

profile of v3, /device:TPU:30, one launch (start us, length us, event | category | flops | bytes accessed | tf_op | source)
XLA Modules:
  0.0 73.3 jit_solution(3606290014131543442)
XLA Ops:
  1.3 70.3 %block.1 = (bf16[2,224,320]{2,1,0:T(8,128)(2,1)S(1)}, bf16[2,2,320,112]{3,2,1,0:T(8,128)(2,1)S(1)}) custom-call(s32[1]{0:T(128)S(6)} %copy.17.ts_ref, s32[2,2,5]{2,1,0:T(2,128)} %ex_ref.1, bf16[2,2,320,112]{3,2,1,0:T(8,128)(2,1)} %bitcast.6, bf16[2,2,320,112]{3,2,1,0:T(8,128)(2,1)} %bitcast.7, f32[320]{0:T(512)} %gain_ref.1, f32[320]{0:T(512)} %bias_ref.1, ...), custom_call_target="tpu_custom_call" | custom-call | tf_op jit(solution)/shard_map/block/pallas_call | solution.py:658
  71.6 0.9 %copy.14 = bf16[2,2,112,320]{2,3,1,0:T(8,128)(2,1)} copy(bf16[2,2,112,320]{3,2,1,0:T(8,128)(2,1)S(1)} %bitcast.5) | data formatting | bytes 573440
  72.5 0.7 copy.16

commit v4 on v3

--- a/solution.py
+++ b/solution.py
@@ -508,7 +508,7 @@
 
     chunk(LAST, all_heads(0, MINE), {})
     give(0)
-    chunk(LAST, all_heads(MINE, BOTH), {2: lambda: take(0)})
+    chunk(LAST, all_heads(MINE, BOTH), {1: lambda: take(0)})
     give(1)
 
     for parity in range(2):

time: 73.4 us -> 73.4 us (level)
  no operation moved by 1% of the time
where the time goes in v4:
time: 73.4 us; the launch traced here: 73.3 us
  Pallas kernels  70.4 us (96%)
  local copies, waits for them, and re-layouts  1.63 us (2%)
  between operations  1.29 us (2%)
    pallas_call x1, Pallas kernels, body(): pl.pallas_call(kernel, out_shape=(pltpu.VMEM((2, BAND, C), BF16), pltpu.V...  70.4 us
    unnamed x2, local copies, waits for them, and re-layouts  1.63 us

profile of v4, /device:TPU:30, one launch (start us, length us, event | category | flops | bytes accessed | tf_op | source)
XLA Modules:
  0.0 73.3 jit_solution(13709606122519717017)
XLA Ops:
  1.3 70.4 %block.1 = (bf16[2,224,320]{2,1,0:T(8,128)(2,1)S(1)}, bf16[2,2,320,112]{3,2,1,0:T(8,128)(2,1)S(1)}) custom-call(s32[1]{0:T(128)S(6)} %copy.17.ts_ref, s32[2,2,5]{2,1,0:T(2,128)} %ex_ref.1, bf16[2,2,320,112]{3,2,1,0:T(8,128)(2,1)} %bitcast.6, bf16[2,2,320,112]{3,2,1,0:T(8,128)(2,1)} %bitcast.7, f32[320]{0:T(512)} %gain_ref.1, f32[320]{0:T(512)} %bias_ref.1, ...), custom_call_target="tpu_custom_call" | custom-call | tf_op jit(solution)/shard_map/block/pallas_call | solution.py:658
  71.7 0.9 %copy.14 = bf16[2,2,112,320]{2,3,1,0:T(8,128)(2,1)} copy(bf16[2,2,112,320]{3,2,1,0:T(8,128)(2,1)S(1)} %bitcast.5) | data formatting | bytes 573440
  72.6 0.7 copy.16
